TPU v7x, 128 devices: a whole 4x4x4 slice. The times are simulated.
128 devices in a mesh: nodes: 128 (over x, z, y, core).
Axes of the slice: x: 4, y: 4, z: 4, core: 2. Of those that a mesh axis runs over, the one named last changes fastest.
Arguments:
- features: bfloat16 [131072, 512], P('nodes'), may hold values from -6 to 6
- preact: float32 [131072, 512], P('nodes'), may hold values from -6 to 6
- cotangent: float32 [131072, 512], P('nodes'), may hold values from -6 to 6
- w_self: float32 [512, 512], replicated, may hold values from -0.25 to 0.25
- w_neigh: float32 [512, 512], replicated, may hold values from -0.25 to 0.25
- tile_counts: int32 [1024, 10, 128, 128], P('nodes'), may hold values from 0 to 2, as said below
- tile_col: int32 [1024, 10], P('nodes'), may hold values from 0 to 71, as said below
- boundary_owner: int32 [128, 64], P('nodes'), may hold values from 0 to 127, as said below
- boundary_slot: int32 [128, 64], P('nodes'), may hold values from 0 to 7
Outputs:
- grad_features: float32 [131072, 512], P('nodes')
- grad_self: float32 [512, 512], replicated
- grad_neigh: float32 [512, 512], replicated
Inputs may be any that keep to these rules, and one draw needn't show every extreme that they name: `tile_col`: values below 8 name one of the device's own blocks, value 8 + k its boundary block k; every boundary block of a device is named by at least one tile of that device's row blocks. `boundary_owner`: the 64 boundary blocks of one device have distinct owners, none of them the device itself. `tile_counts`: most entries are zero.
All inputs are finite; a program needn't handle non-finite values.
Results may differ from a plain program's by a relative error of at most 0.007.
Values may be sent and summed in bfloat16 or wider, within the bound.
No kernel may reach another device: no remote copies, remote signals or barrier semaphores. Data moves between devices by JAX's collectives and lax.ppermute only.
A program may use at most 256 MiB of HBM per device.

v0:
```python
import math

import jax
import jax.numpy as jnp
from jax import lax
from jax.sharding import PartitionSpec as P

PRECISE = lax.Precision.HIGHEST


def normalized_tiles(counts):
    values = counts.astype(jnp.float32)
    degree = 1.0 + jnp.sum(values, axis=(1, 3))
    return values / jnp.sqrt(degree)[:, None, :, None]


def split_parts(values):
    upper = values.astype(jnp.bfloat16)
    lower = (values - upper.astype(jnp.float32)).astype(jnp.bfloat16)
    return (upper, lower)


def shards(
    features,
    preact,
    cotangent,
    w_self,
    w_neigh,
    tile_counts,
    tile_col,
    boundary_owner,
    boundary_slot,
):
    device_count = lax.axis_size("nodes")
    own_blocks = tile_counts.shape[0]
    block_rows = tile_counts.shape[2]
    feature_width = features.shape[1]
    remote_count = boundary_owner.shape[1]
    total_nodes = features.shape[0] * device_count
    grad_pre = jnp.where(preact > 0, cotangent, jnp.zeros_like(cotangent))
    weights = normalized_tiles(tile_counts)
    owner_list = boundary_owner[0]
    slot_list = boundary_slot[0]
    peer_ids = jnp.arange(device_count, dtype=jnp.int32)
    matches = owner_list[None, :] == peer_ids[:, None]
    wanted = jnp.sum(jnp.where(matches, slot_list[None, :] + 1, 0), axis=1) - 1
    asked = lax.all_to_all(wanted, "nodes", split_axis=0, concat_axis=0, tiled=True)
    present = asked >= 0
    local_blocks = features.reshape(own_blocks, block_rows, feature_width)
    outgoing = jnp.where(
        present[:, None, None], local_blocks[jnp.maximum(asked, 0)], jnp.zeros((), jnp.bfloat16)
    )
    back_neigh = jnp.dot(grad_pre, w_neigh.T, precision=PRECISE).reshape(
        own_blocks, block_rows, feature_width
    )
    contrib = jnp.einsum("bkij,bid->bkjd", weights, back_neigh, precision=PRECISE)
    contrib_upper, contrib_lower = split_parts(contrib)
    column_ids = jnp.arange(own_blocks + remote_count, dtype=jnp.int32)
    one_hot = (tile_col[:, :, None] == column_ids[None, None, :]).astype(jnp.bfloat16)
    binned = jnp.einsum("bkc,bkjd->cjd", one_hot, contrib_upper, preferred_element_type=jnp.float32)
    binned = binned + jnp.einsum(
        "bkc,bkjd->cjd", one_hot, contrib_lower, preferred_element_type=jnp.float32
    )
    remote_part = binned[own_blocks:].astype(jnp.bfloat16)
    returning = (
        jnp.zeros((device_count, block_rows, feature_width), jnp.bfloat16)
        .at[owner_list]
        .set(remote_part)
    )
    owner_hot = (asked[:, None] == jnp.arange(own_blocks, dtype=jnp.int32)[None, :]).astype(
        jnp.bfloat16
    )
    received = lax.all_to_all(outgoing, "nodes", split_axis=0, concat_axis=0, tiled=True)
    summed = jnp.einsum(
        "rb,rjd->bjd",
        owner_hot,
        lax.all_to_all(returning, "nodes", split_axis=0, concat_axis=0, tiled=True),
        preferred_element_type=jnp.float32,
    )
    fetched = received[owner_list]
    lookup = jnp.concatenate([local_blocks, fetched], axis=0)
    gathered = lookup[tile_col]
    weight_upper, weight_lower = split_parts(weights)
    aggregated = jnp.einsum(
        "bkij,bkjd->bid", weight_upper, gathered, preferred_element_type=jnp.float32
    )
    aggregated = aggregated + jnp.einsum(
        "bkij,bkjd->bid", weight_lower, gathered, preferred_element_type=jnp.float32
    )
    aggregated = aggregated.reshape(-1, feature_width)
    self_term = jnp.dot(features.astype(jnp.float32).T, grad_pre, precision=PRECISE)
    neigh_term = jnp.dot(aggregated.T, grad_pre, precision=PRECISE)
    self_total, neigh_total = lax.psum((self_term, neigh_term), "nodes")
    norm_factor = 1.0 / math.sqrt(total_nodes)
    local_sum = (binned[:own_blocks] + summed).reshape(-1, feature_width)
    grad_features = jnp.dot(grad_pre, w_self.T, precision=PRECISE) + local_sum
    return (grad_features, self_total * norm_factor, neigh_total * norm_factor)


def solution(mesh):
    return jax.shard_map(
        shards,
        mesh=mesh,
        in_specs=(
            P("nodes", None),
            P("nodes", None),
            P("nodes", None),
            P(),
            P(),
            P("nodes", None, None, None),
            P("nodes", None),
            P("nodes", None),
            P("nodes", None),
        ),
        out_specs=(P("nodes", None), P(), P()),
        check_vma=False,
    )
```

profile of v0, /device:TPU:1, one launch (start us, length us, event | category | flops | bytes accessed | tf_op | source)
XLA Modules:
  0.0 659.4 jit_solution(1403533815016173599)
XLA Ops:
  7.2 0.0 copy-start
  7.2 0.7 add_bitcast_fusion.1
  7.9 0.7 select_reduce_fusion
  8.7 0.1 copy.53
  8.8 20.8 %all_to_all.16 = s32[128,1,1]{2,1,0:T(1,128)S(1)} all-to-all(s32[128,1,1]{2,1,0:T(1,128)S(1)} %copy.53), channel_id=1, replica_groups=mesh['nodes'=128] {'nodes'}, dimensions={0} | all-to-all | bytes 1024 | tf_op jit(solution)/shard_map/all_to_all | solution.py:47
  29.6 4.7 maximum_reduce_fusion
  34.3 9.4 %gather_fusion = bf16[128,128,512]{2,1,0:T(8,128)(2,1)} fusion(bf16[8,128,512]{2,1,0:T(8,128)(2,1)} %bitcast.51, s32[1024]{0:T(1024)S(1)} %pad_clamp_fusion.2), kind=kCustom, calls=%fused_computation | custom fusion | bytes 33554944 | tf_op jit(solution)/shard_map/gather | solution.py:51
  43.7 2.4 compare_reduce_fusion
  46.0 14.0 %broadcast_select_fusion = bf16[128,128,512]{2,1,0:T(8,128)(2,1)} fusion(bf16[128,128,512]{2,1,0:T(8,128)(2,1)} %gather_fusion, pred[128]{0:T(512)(128)(4,1)S(1)} %compare_reduce_fusion), kind=kLoop, calls=%fused_computation.13 | loop fusion | flops 8388608 | bytes 33554560 | tf_op jit(solution)/shard_map/jit(_where)/select_n | solution.py:50
  60.0 6.0 all-to-all-start.2
  66.1 0.0 copy-start.5
  66.1 3.1 convert_reduce_fusion
  69.2 0.0 slice-start
  69.2 0.0 copy-done.4
  69.2 0.6 copy-done.5
  69.9 0.5 compare_select_fusion
  70.4 3.5 fusion.24
  73.9 0.0 copy-start.7
  73.9 23.5 %subtract_convert_fusion = (bf16[8,10,128,512]{3,2,1,0:T(8,128)(2,1)}, bf16[8,10,128,512]{3,2,1,0:T(8,128)(2,1)}) fusion(f32[8,128,512,1]{2,1,3,0:T(8,128)S(1)} %bitcast.58, s32[8,10,128,128]{3,2,1,0:T(8,128)S(1)} %bitcast.56, f32[8,128]{1,0:T(8,128)S(1)} %add_sqrt_fusion), kind=kOutput, calls=%fused_computation.4 | convolution fusion | flops 8076656640 | bytes 28315648 | tf_op jit(solution)/shard_map/bkij,bid->bkjd/dot_general | solution.py:56
  97.4 24.2 %fusion.2 = f32[72,128,512,1]{2,0,3,1:T(8,128)} fusion(bf16[8,10,128,512]{3,2,1,0:T(8,128)(2,1)} %get-tuple-element.22, s32[8,10]{1,0:T(8,128)S(1)} %copy-done.7), kind=kOutput, calls=%fused_computation.9 | convolution fusion | flops 754980480 | bytes 29360448 | tf_op jit(solution)/shard_map/bkc,bkjd->cjd/dot_general | solution.py:61
  121.6 28.1 %bitcast_add_fusion = f32[72,128,512]{2,0,1:T(8,128)} fusion(f32[72,128,512,1]{2,0,3,1:T(8,128)} %fusion.2, bf16[8,10,128,512]{3,2,1,0:T(8,128)(2,1)} %get-tuple-element.23, s32[8,10]{1,0:T(8,128)S(1)} %copy-done.7), kind=kOutput, calls=%fused_computation.5 | convolution fusion | flops 759699072 | bytes 48234816 | tf_op jit(solution)/shard_map/bkc,bkjd->cjd/dot_general | solution.py:60
  149.8 9.2 %slice.19 = bf16[64,128,512]{2,0,1:T(8,128)(2,1)} slice(f32[72,128,512]{2,0,1:T(8,128)} %bitcast_add_fusion), slice={[8:72], [0:128], [0:512]} | slice | bytes 16777216 | tf_op jit(solution)/shard_map/slice | solution.py:64
  159.0 0.0 copy-start.8
  159.0 11.4 %copy.54 = bf16[64,128,512]{2,1,0:T(8,128)(2,1)} copy(bf16[64,128,512]{2,0,1:T(8,128)(2,1)} %slice.19) | data formatting | bytes 16777216 | tf_op jit(solution)/shard_map/slice | solution.py:64
  170.5 5.9 broadcast_in_dim.45
  176.4 22.1 %scatter_fusion = bf16[128,128,512]{2,1,0:T(8,128)(2,1)} fusion(bf16[128,128,512]{2,1,0:T(8,128)(2,1)} %broadcast_in_dim.45, s32[64]{0:T(128)S(1)} %fusion.22, bf16[64,128,512]{2,1,0:T(8,128)(2,1)} %copy.54), kind=kCustom, calls=%fused_computation.3 | custom fusion | bytes 25166080 | tf_op jit(solution)/shard_map/scatter | solution.py:68
  198.5 98.6 %all-to-all-done.2 = bf16[128,128,512]{2,1,0:T(8,128)(2,1)} async-done(((bf16[128,128,512]{2,1,0:T(8,128)(2,1)}), bf16[128,128,512]{2,1,0:T(8,128)(2,1)}, u32[]{:S(2)}, u32[]{:S(2)}) %all-to-all-start.2) | async-done | bytes 16777248 | tf_op jit(solution)/shard_map/all_to_all | solution.py:73
  297.1 18.0 %all-to-all-start.1 = ((bf16[128,128,512]{2,1,0:T(8,128)(2,1)}), bf16[128,128,512]{2,1,0:T(8,128)(2,1)}, u32[]{:S(2)}, u32[]{:S(2)}) async-start(bf16[128,128,512]{2,1,0:T(8,128)(2,1)} %scatter_fusion), calls=%async_computation.1 | async-start | bytes 33554432 | tf_op jit(solution)/shard_map/all_to_all | solution.py:77
  315.1 0.0 all-reduce.3.cloned.1.call-start
  315.2 0.1 reshape.98
  315.3 2.8 convolution_bitcast_fusion
  318.1 11.4 %gather_fusion.1 = bf16[64,128,512]{2,1,0:T(8,128)(2,1)} fusion(bf16[128,128,512]{2,1,0:T(8,128)(2,1)} %all-to-all-done.2, s32[1024]{0:T(1024)S(1)} %pad_clamp_fusion.1), kind=kCustom, calls=%fused_computation.1 | custom fusion | bytes 16777472 | tf_op jit(solution)/shard_map/gather | solution.py:80
  329.5 7.9 %pad_maximum_fusion = bf16[72,128,512]{2,1,0:T(8,128)(2,1)} fusion(bf16[64,128,512]{2,1,0:T(8,128)(2,1)} %gather_fusion.1, bf16[8,128,512]{2,1,0:T(8,128)(2,1)S(1)} %bitcast.52), kind=kLoop, calls=%fused_computation.14 | loop fusion | flops 4718592 | bytes 18874368 | tf_op jit(solution)/shard_map/concatenate | solution.py:81
  337.4 9.9 %gather_fusion.2 = bf16[80,128,512]{2,1,0:T(8,128)(2,1)} fusion(bf16[72,128,512]{2,1,0:T(8,128)(2,1)} %pad_maximum_fusion, s32[1024]{0:T(1024)S(1)} %pad_clamp_fusion), kind=kCustom, calls=%fused_computation.2 | custom fusion | bytes 20971840 | tf_op jit(solution)/shard_map/gather | solution.py:82
  347.3 6.8 %fusion.12 = f32[8,128,512,1]{2,1,3,0:T(8,128)S(1)} fusion(bf16[8,10,128,512]{3,2,1,0:T(8,128)(2,1)} %bitcast.53, s32[8,10,128,128]{3,2,1,0:T(8,128)} %param.14, f32[8,128]{1,0:T(8,128)S(1)} %add_sqrt_fusion), kind=kOutput, calls=%fused_computation.25 | convolution fusion | flops 1346109440 | bytes 17829888 | tf_op jit(solution)/shard_map/bkij,bkjd->bid/dot_general | solution.py:84
  354.1 1.7 copy-done.3
  355.9 4.1 bitcast_add_fusion.1
  359.9 4.5 fusion.25
  364.4 0.0 all-reduce.3.cloned.1.call-update
  364.4 181.5 %all-to-all-done.1 = bf16[128,128,512]{2,1,0:T(8,128)(2,1)} async-done(((bf16[128,128,512]{2,1,0:T(8,128)(2,1)}), bf16[128,128,512]{2,1,0:T(8,128)(2,1)}, u32[]{:S(2)}, u32[]{:S(2)}) %all-to-all-start.1) | async-done | bytes 16777248 | tf_op jit(solution)/shard_map/all_to_all | solution.py:77
  546.0 24.2 %slice_add_fusion = f32[8,128,512]{2,0,1:T(8,128)S(1)} fusion(f32[72,128,512]{2,0,1:T(8,128)} %bitcast_add_fusion, bf16[128,128,512]{2,1,0:T(8,128)(2,1)} %all-to-all-done.1, s32[128]{0:T(128)S(1)} %get-tuple-element.19), kind=kOutput, calls=%fused_computation.19 | convolution fusion | flops 134743040 | bytes 20972032 | tf_op jit(solution)/shard_map/rb,rjd->bjd/dot_general | solution.py:74
  570.1 1.2 copy.56
  571.4 0.0 copy-start.1
  571.4 5.1 bitcast_add_fusion.2
  576.4 71.5 %all-reduce.3.cloned.1.call-done = (f32[512,512]{0,1:T(8,128)}, f32[512,512]{0,1:T(8,128)}) async-done(((f32[512,512]{0,1:T(8,128)}, f32[512,512]{0,1:T(8,128)}), (f32[512,512]{0,1:T(8,128)}, f32[512,512]{0,1:T(8,128)})) %all-reduce.3.cloned.1.call-update) | async-done | bytes 2097168 | tf_op jit(solution)/shard_map/psum | solution.py:93
  647.9 1.8 broadcast_multiply_fusion
  649.7 1.3 copy.58
  651.0 1.3 copy.59
  (21 shorter events, 0.1 us)
Async XLA Ops:
  7.2 63.2 %copy-start = (f32[512,512]{1,0:T(8,128)S(1)}, f32[512,512]{1,0:T(8,128)}, u32[]{:S(2)}) copy-start(f32[512,512]{1,0:T(8,128)} %param.13) | copy-start | bytes 3145732
  60.0 237.1 %all-to-all-start.2 = ((bf16[128,128,512]{2,1,0:T(8,128)(2,1)}), bf16[128,128,512]{2,1,0:T(8,128)(2,1)}, u32[]{:S(2)}, u32[]{:S(2)}) async-start(bf16[128,128,512]{2,1,0:T(8,128)(2,1)} %broadcast_select_fusion), calls=%async_computation.2 | async-start | bytes 33554432 | tf_op jit(solution)/shard_map/all_to_all | solution.py:73
  66.1 3.1 copy-start.4
  66.1 3.8 copy-start.5
  69.2 4.7 slice-start
  69.9 4.0 slice-start.1
  73.9 23.5 %copy-start.7 = (s32[8,10]{1,0:T(8,128)S(1)}, s32[8,10]{1,0:T(8,128)}, u32[]{:S(2)}) copy-start(s32[8,10]{1,0:T(8,128)} %param.15) | copy-start | bytes 964
  159.0 11.5 %copy-start.8 = (s32[1,64]{1,0:T(1,128)S(1)}, s32[1,64]{1,0:T(1,128)}, u32[]{:S(2)}) copy-start(s32[1,64]{1,0:T(1,128)} %param.16) | copy-start | bytes 772
  198.5 116.8 %copy-start.2 = (bf16[1024,512]{1,0:T(8,128)(2,1)S(1)}, bf16[1024,512]{1,0:T(8,128)(2,1)}, u32[]{:S(2)}) copy-start(bf16[1024,512]{1,0:T(8,128)(2,1)} %param.9) | copy-start | bytes 3145732
  297.1 248.8 %all-to-all-start.1 = ((bf16[128,128,512]{2,1,0:T(8,128)(2,1)}), bf16[128,128,512]{2,1,0:T(8,128)(2,1)}, u32[]{:S(2)}, u32[]{:S(2)}) async-start(bf16[128,128,512]{2,1,0:T(8,128)(2,1)} %scatter_fusion), calls=%async_computation.1 | async-start | bytes 33554432 | tf_op jit(solution)/shard_map/all_to_all | solution.py:77
  315.1 332.8 %all-reduce.3.cloned.1.call-start = ((), (), s32[]{:S(2)}) async-start(), calls=%async_computation.3 | async-start | bytes 4194304 | tf_op jit(solution)/shard_map/psum | solution.py:93
  347.3 8.5 %copy-start.3 = (bf16[80,128,512]{2,1,0:T(8,128)(2,1)S(1)}, bf16[80,128,512]{2,1,0:T(8,128)(2,1)}, u32[]{:S(2)}) copy-start(bf16[80,128,512]{2,1,0:T(8,128)(2,1)} %gather_fusion.2) | copy-start | bytes 31457284
  546.0 25.4 %copy-start.6 = (f32[512,512]{1,0:T(8,128)S(1)}, f32[512,512]{1,0:T(8,128)}, u32[]{:S(2)}) copy-start(f32[512,512]{1,0:T(8,128)} %param.12) | copy-start | bytes 3145732
  571.4 81.0 %copy-start.1 = (f32[512,512]{1,0:T(8,128)S(1)}, f32[512,512]{1,0:T(8,128)}, u32[]{:S(2)}) copy-start(f32[512,512]{1,0:T(8,128)} %param.13) | copy-start | bytes 3145732
Sparse Core Ops, SparseCore 0:
  364.6 283.3 all-reduce.2
where the time goes:
time: 669 us; the launch traced here: 659 us
  waiting for transfers between devices  352 us (53%)
  matrix products  127 us (19%)
  local copies, waits for them, and re-layouts  85.9 us (13%)
  other arithmetic  35.8 us (5%)
  starting transfers between devices  24.1 us (4%)
  blocking collectives  20.8 us (3%)
  between operations  14.5 us (2%)
    all_to_all x1, waiting for transfers between devices, shards(): lax.all_to_all(returning, 'nodes', split_axis=0, concat_axis=0, tiled=True)  182 us
    all_to_all x1, waiting for transfers between devices, shards(): lax.all_to_all(outgoing, 'nodes', split_axis=0, concat_axis=0, tiled=True)  98.6 us
    psum x1, waiting for transfers between devices, shards(): self_total, neigh_total = lax.psum((self_term, neigh_term), 'nodes')  71.5 us
    dot_general x1, matrix products, shards(): jnp.einsum('bkc,bkjd->cjd', one_hot, contrib_upper, preferred_element_typ...  28.1 us
    dot_general x1, matrix products, shards(): jnp.einsum('bkc,bkjd->cjd', one_hot, contrib_lower, preferred_element_typ...  24.2 us
    dot_general x1, matrix products, shards(): jnp.einsum('rb,rjd->bjd', owner_hot, lax.all_to_all(returning, 'nodes', s...  24.2 us
    dot_general x1, matrix products, shards(): jnp.einsum('bkij,bid->bkjd', weights, back_neigh, precision=PRECISE)  23.5 us
    scatter x1, local copies, waits for them, and re-layouts, shards(): returning = jnp.zeros((device_count, block_rows, feature_width), jnp.bflo...  22.1 us
  transfers between devices with their start and end apart: 3, of which 3 were waited for; matrix products, arithmetic and copies ran while one was open for 32% of the time, Pallas kernels for 0%

commit v1 on v0

v1 whole, which is shorter than its diff:
```python
import functools
import math

import jax
import jax.numpy as jnp
from jax import lax
from jax.experimental import pallas as pl
from jax.experimental.pallas import tpu as pltpu
from jax.sharding import PartitionSpec as P

D = 512
BLK = 128
BLK_DEV = 8
OWNERS = 128
NB = 64
K = 10
COLUMNS = BLK_DEV + NB
F32 = jnp.float32
BF16 = jnp.bfloat16


def dot(a, b):
    return lax.dot_general(a, b, (((1,), (0,)), ((), ())), preferred_element_type=F32)


def halves(values):
    upper = values.astype(BF16)
    return upper, (values - upper.astype(F32)).astype(BF16)


def scatter_kernel(col_ref, owner_ref, counts_ref, preact_ref, cot_ref, own_ref, send_ref, acc, stage, sems):
    b = pl.program_id(0)

    @pl.when(b == 0)
    def _():
        acc[...] = jnp.zeros_like(acc)

    counts = counts_ref[0].astype(F32)
    degree = 1.0 + jnp.sum(jnp.sum(counts, axis=0), axis=1, keepdims=True)
    grad = jnp.where(preact_ref[...] > 0, cot_ref[...], 0.0) / jnp.sqrt(degree)
    upper, lower = halves(grad.T)
    both = jnp.concatenate([upper, lower], axis=1)
    tiles = counts.astype(BF16)
    for t in range(0, K, 2):
        pair = jnp.concatenate([tiles[t], tiles[t + 1]], axis=1)
        part = dot(both, jnp.concatenate([pair, pair], axis=0))
        acc[col_ref[b, t]] += part[:, :BLK]
        acc[col_ref[b, t + 1]] += part[:, BLK:]

    @pl.when(b == BLK_DEV - 1)
    def _():
        own_ref[...] = acc[:BLK_DEV]

        def put(k):
            return pltpu.make_async_copy(stage.at[k], send_ref.at[owner_ref[k]], sems.at[k])

        @pl.loop(0, NB)
        def _(k):
            stage[k] = acc[BLK_DEV + k].astype(BF16)
            put(k).start()

        @pl.loop(0, NB)
        def _(k):
            put(k).wait()


def partials(tile_col, owners, counts, preact, cotangent):
    return pl.pallas_call(
        scatter_kernel,
        grid_spec=pltpu.PrefetchScalarGridSpec(
            num_scalar_prefetch=2,
            grid=(BLK_DEV,),
            in_specs=[
                pl.BlockSpec((1, K, BLK, BLK), lambda b, *_: (b, 0, 0, 0)),
                pl.BlockSpec((BLK, D), lambda b, *_: (b, 0)),
                pl.BlockSpec((BLK, D), lambda b, *_: (b, 0)),
            ],
            out_specs=[
                pl.BlockSpec((BLK_DEV, D, BLK), lambda b, *_: (0, 0, 0)),
                pl.BlockSpec(memory_space=pl.ANY),
            ],
            scratch_shapes=[
                pltpu.VMEM((COLUMNS, D, BLK), F32),
                pltpu.VMEM((NB, D, BLK), BF16),
                pltpu.SemaphoreType.DMA((NB,)),
            ],
        ),
        out_shape=[
            jax.ShapeDtypeStruct((BLK_DEV, D, BLK), F32),
            jax.ShapeDtypeStruct((OWNERS, D, BLK), BF16),
        ],
        compiler_params=pltpu.CompilerParams(vmem_limit_bytes=56 << 20),
        cost_estimate=pl.CostEstimate(
            flops=4 * BLK_DEV * K * BLK * BLK * D, bytes_accessed=20 << 20, transcendentals=0
        ),
    )(tile_col, owners, counts, preact, cotangent)


GROUP = 8


def gather_kernel(asked_ref, recv_ref, own_ref, base_ref, feat_ref, weight_ref, grad_ref, neigh_ref, acc):
    step = pl.program_id(0)

    @pl.when(step == 0)
    def _():
        acc[...] = own_ref[...]

    for i in range(GROUP):
        slot = asked_ref[step * GROUP + i]

        @pl.when(slot >= 0)
        def _():
            acc[slot] += recv_ref[i].astype(F32)

    @pl.when(step == OWNERS // GROUP - 1)
    def _():
        w_upper, w_lower = halves(weight_ref[...])
        neigh_ref[...] = jnp.zeros_like(neigh_ref)
        for g in range(0, BLK_DEV, 2):
            total = jnp.concatenate([acc[g], acc[g + 1]], axis=1)
            upper, lower = halves(total)
            rows = slice(g * BLK, (g + 2) * BLK)
            feat = feat_ref[rows, :]
            neigh_ref[...] += dot(upper, feat) + dot(lower, feat)
            upper, lower = halves(total.T)
            grad_ref[rows, :] = base_ref[rows, :] + (
                dot(upper, w_upper) + dot(lower, w_upper) + dot(upper, w_lower)
            )


def totals(asked, received, own, base, features, weight):
    whole = lambda *shape: pl.BlockSpec(shape, lambda s, *_: (0,) * len(shape))
    return pl.pallas_call(
        gather_kernel,
        grid_spec=pltpu.PrefetchScalarGridSpec(
            num_scalar_prefetch=1,
            grid=(OWNERS // GROUP,),
            in_specs=[
                pl.BlockSpec((GROUP, D, BLK), lambda s, *_: (s, 0, 0)),
                whole(BLK_DEV, D, BLK),
                whole(BLK_DEV * BLK, D),
                whole(BLK_DEV * BLK, D),
                whole(D, D),
            ],
            out_specs=[whole(BLK_DEV * BLK, D), whole(D, D)],
            scratch_shapes=[pltpu.VMEM((BLK_DEV, D, BLK), F32)],
        ),
        out_shape=[
            jax.ShapeDtypeStruct((BLK_DEV * BLK, D), F32),
            jax.ShapeDtypeStruct((D, D), F32),
        ],
        compiler_params=pltpu.CompilerParams(vmem_limit_bytes=48 << 20),
        cost_estimate=pl.CostEstimate(
            flops=10 * BLK_DEV * BLK * D * D, bytes_accessed=26 << 20, transcendentals=0
        ),
    )(asked, received, own, base, features, weight)


def sum_everywhere(values):
    rows = D // OWNERS
    shares = lax.all_to_all(values.reshape(OWNERS, rows, D), "nodes", 0, 0, tiled=True)
    share = jnp.sum(shares, axis=0)
    spread = jnp.broadcast_to(share[None], (OWNERS, rows, D))
    return lax.all_to_all(spread, "nodes", 0, 0, tiled=True).reshape(D, D)


def shards(features, preact, cotangent, w_self, w_neigh, tile_counts, tile_col, owner, slot):
    me = lax.axis_index("nodes")
    lists = lax.all_gather(owner * BLK_DEV + slot, "nodes", axis=0, tiled=True)
    own, outgoing = partials(tile_col, owner[0], tile_counts, preact, cotangent)
    received = lax.all_to_all(outgoing, "nodes", 0, 0, tiled=True)

    asked = jnp.max(jnp.where(lists // BLK_DEV == me, lists % BLK_DEV, -1), axis=1)
    grad_pre = jnp.where(preact > 0, cotangent, 0.0)
    upper, lower = halves(grad_pre)
    w_upper, w_lower = halves(w_self.T)
    base = dot(upper, w_upper) + dot(lower, w_upper) + dot(upper, w_lower)
    turned = features.T
    self_part = dot(turned, upper) + dot(turned, lower)
    self_total = lax.psum(self_part, "nodes")

    grad_features, neigh_part = totals(asked, received, own, base, features, w_neigh.T)
    neigh_total = sum_everywhere(neigh_part).T
    scale = 1.0 / math.sqrt(OWNERS * BLK_DEV * BLK)
    return grad_features, self_total * scale, neigh_total * scale


def solution(mesh):
    rows = P("nodes", None)
    return jax.shard_map(
        shards,
        mesh=mesh,
        in_specs=(rows, rows, rows, P(), P(), P("nodes", None, None, None), rows, rows, rows),
        out_specs=(rows, P(), P()),
        check_vma=False,
    )
```

time: 669 us -> 523 us (0.78); the launches traced: 659 us -> 522 us
  blocking collectives: 20.8 us -> 261 us
  waiting for transfers between devices: 352 us -> 170 us
  matrix products: 127 us -> 8.18 us
  local copies, waits for them, and re-layouts: 85.9 us -> 10.9 us
  Pallas kernels: 0 us -> 33.6 us
  other arithmetic: 35.8 us -> 4.2 us
    all_to_all x2 -> x3, waiting for transfers between devices: 280 us -> 17.5 us  [the longest x1 17.5 us: sum_everywhere(): lax.all_to_all(values.reshape(OWNERS, rows, D), 'nodes', 0, 0, tiled=True)]
    all_gather x0 -> x1, blocking collectives: none -> 261 us  [shards(): lists = lax.all_gather(owner * BLK_DEV + slot, 'nodes', axis=0, tiled=True)]
    dot_general x10 -> x5, matrix products: 127 us -> 8.18 us  [dot(): lax.dot_general(a, b, (((1,), (0,)), ((), ())), preferred_element_type=F32)]
    psum x1, waiting for transfers between devices: 71.5 us -> 152 us  [shards(): self_total = lax.psum(self_part, 'nodes')]
    pallas_call x0 -> x2, Pallas kernels: none -> 33.6 us  [the longest x1 17.3 us: totals(): pl.pallas_call(gather_kernel, grid_spec=pltpu.PrefetchScalarGridSpec(num_...]
    gather x3 -> x0, local copies, waits for them, and re-layouts: 30.7 us -> none  [the longest x1 11.4 us: shards(): fetched = received[owner_list]]
    scatter x1 -> x0, local copies, waits for them, and re-layouts: 22.1 us -> none  [shards(): returning = jnp.zeros((device_count, block_rows, feature_width), jnp.bflo...]
    all_to_all x1 -> x0, blocking collectives: 20.8 us -> none  [shards(): lax.all_to_all(wanted, 'nodes', split_axis=0, concat_axis=0, tiled=True)]
  transfers between devices with their start and end apart: 3 -> 4, of which waited for: 3 -> 2; matrix products, arithmetic and copies ran while one was open for 32% -> 3% of each run, Pallas kernels for 0% -> 0%
where the time goes in v1:
time: 523 us; the launch traced here: 522 us
  blocking collectives  261 us (50%)
  waiting for transfers between devices  170 us (33%)
  Pallas kernels  33.6 us (6%)
  starting transfers between devices  20.3 us (4%)
  between operations  14.2 us (3%)
  local copies, waits for them, and re-layouts  10.9 us (2%)
  matrix products  8.18 us (2%)
    all_gather x1, blocking collectives, shards(): lists = lax.all_gather(owner * BLK_DEV + slot, 'nodes', axis=0, tiled=True)  261 us
    psum x1, waiting for transfers between devices, shards(): self_total = lax.psum(self_part, 'nodes')  152 us
    all_to_all x1, waiting for transfers between devices, sum_everywhere(): lax.all_to_all(values.reshape(OWNERS, rows, D), 'nodes', 0, 0, tiled=True)  17.5 us
    pallas_call x1, Pallas kernels, totals(): pl.pallas_call(gather_kernel, grid_spec=pltpu.PrefetchScalarGridSpec(num_...  17.3 us
    pallas_call x1, Pallas kernels, partials(): pl.pallas_call(scatter_kernel, grid_spec=pltpu.PrefetchScalarGridSpec(num...  16.3 us
    all_to_all x1, starting transfers between devices, shards(): received = lax.all_to_all(outgoing, 'nodes', 0, 0, tiled=True)  12 us
  transfers between devices with their start and end apart: 4, of which 2 were waited for; matrix products, arithmetic and copies ran while one was open for 3% of the time, Pallas kernels for 0%

profile of v1, /device:TPU:1, one launch (start us, length us, event | category | flops | bytes accessed | tf_op | source)
XLA Modules:
  0.0 522.3 jit_solution(1392642255694674502)
XLA Ops:
  7.2 16.3 %shard_map.112 = (f32[8,512,128]{2,1,0:T(8,128)}, bf16[128,512,128]{2,1,0:T(8,128)(2,1)}) custom-call(s32[8,10]{1,0:T(8,128)} %col_ref.1, s32[64]{0:T(128)} %bitcast.47, s32[8,10,128,128]{3,2,1,0:T(8,128)} %counts_ref.1, f32[1024,512]{1,0:T(8,128)} %preact_ref.1, f32[1024,512]{1,0:T(8,128)} %cot_ref.1), custom_call_target="tpu_custom_call" | custom-call | flops 2684354560 | bytes 20971520 | tf_op jit(solution)/shard_map/pallas_call | solution.py:68
  23.5 12.0 %all-to-all-start = ((bf16[128,512,128]{2,1,0:T(8,128)(2,1)}), bf16[128,512,128]{2,1,0:T(8,128)(2,1)}, u32[]{:S(2)}, u32[]{:S(2)}) async-start(bf16[128,512,128]{2,1,0:T(8,128)(2,1)} %get-tuple-element.7), calls=%async_computation | async-start | bytes 33554432 | tf_op jit(solution)/shard_map/all_to_all | solution.py:172
  35.5 0.0 copy-start.9
  35.5 0.0 copy-start.10
  35.5 0.0 copy-start.8
  35.5 1.7 copy.17
  37.2 0.0 copy-done.9
  37.2 0.0 copy-done.10
  37.3 261.2 %all-gather = s32[128,1,64]{2,1,0:T(1,128)S(1)} all-gather(s32[1,1,64]{2,1,0:T(1,128)S(1)} %add_bitcast_fusion), channel_id=1, replica_groups=mesh['nodes'=128] {'nodes'}, dimensions={0}, use_global_device_ids=true | all-gather | bytes 33024 | tf_op jit(solution)/shard_map/all_gather | solution.py:170
  298.5 0.1 fusion.6.asked_ref
  298.6 0.0 copy-done.8
  298.6 0.0 copy-start.4
  298.6 2.2 subtract_convert_fusion
  300.9 0.0 copy-start.7
  300.9 0.0 copy-start.5
  300.9 0.0 copy-done.4
  300.9 0.7 fusion.14
  301.6 0.2 copy-done.7
  301.8 0.7 fusion.16
  302.6 0.0 copy-done.5
  302.6 0.0 copy-start
  302.6 2.1 add_add_fusion.base_ref
  304.7 0.0 all-to-all-done.recv_ref
  304.7 0.0 copy-done
  304.7 0.0 copy-start.1
  304.7 1.2 copy-done.1
  305.9 17.3 %shard_map.113 = (f32[1024,512]{1,0:T(8,128)}, f32[512,512]{1,0:T(8,128)S(1)}) custom-call(s32[128]{0:T(128)S(1)} %fusion.6.asked_ref, bf16[128,512,128]{2,1,0:T(8,128)(2,1)} %all-to-all-done.recv_ref, f32[8,512,128]{2,1,0:T(8,128)S(1)} %copy-done, f32[1024,512]{1,0:T(8,128)} %add_add_fusion.base_ref, bf16[1024,512]{1,0:T(8,128)(2,1)S(1)} %copy-done.1, ...), custom_call_target="tpu_custom_call" | custom-call | flops 2684354560 | bytes 27262976 | tf_op jit(solution)/shard_map/pallas_call | solution.py:134
  323.2 1.0 copy-done.3
  324.2 2.7 reshape.13
  326.9 3.6 all-to-all-start.1
  330.5 0.0 copy-done.2
  330.5 0.0 copy-done.6
  330.5 1.7 fusion.20
  332.2 17.5 %all-to-all-done.1 = f32[128,4,512]{2,1,0:T(4,128)S(1)} async-done(((f32[128,4,512]{2,1,0:T(4,128)}), f32[128,4,512]{2,1,0:T(4,128)S(1)}, u32[]{:S(2)}, u32[]{:S(2)}) %all-to-all-start.1) | async-done | bytes 1048608 | tf_op jit(solution)/shard_map/all_to_all | solution.py:162
  349.7 0.2 reduce_sum.9
  349.9 1.1 broadcast_in_dim.6
  351.0 4.7 all-to-all-start.2
  355.7 0.0 all-reduce.2.cloned.1.call-start
  355.8 0.0 copy-done.11
  355.8 2.9 fusion
  358.7 0.0 all-reduce.2.cloned.1.call-update
  358.7 152.1 %all-reduce.2.cloned.1.call-done = f32[512,512]{0,1:T(8,128)} async-done(((f32[512,512]{0,1:T(8,128)}), f32[512,512]{0,1:T(8,128)}) %all-reduce.2.cloned.1.call-update) | async-done | bytes 1048592 | tf_op jit(solution)/shard_map/psum | solution.py:181
  510.8 1.3 broadcast_multiply_fusion.1
  512.2 1.3 copy.18
  513.5 0.0 all-to-all-done.2
  513.5 0.3 broadcast_multiply_fusion
  513.8 0.4 mul.22
  514.1 1.3 copy.19
  (5 shorter events, 0.0 us)
Async XLA Ops:
  23.5 281.2 %all-to-all-start = ((bf16[128,512,128]{2,1,0:T(8,128)(2,1)}), bf16[128,512,128]{2,1,0:T(8,128)(2,1)}, u32[]{:S(2)}, u32[]{:S(2)}) async-start(bf16[128,512,128]{2,1,0:T(8,128)(2,1)} %get-tuple-element.7), calls=%async_computation | async-start | bytes 33554432 | tf_op jit(solution)/shard_map/all_to_all | solution.py:172
  35.5 1.8 copy-start.9
  35.5 1.8 copy-start.10
  35.5 263.1 %copy-start.8 = (f32[1024,512]{1,0:T(8,128)S(1)}, f32[1024,512]{1,0:T(8,128)}, u32[]{:S(2)}) copy-start(f32[1024,512]{1,0:T(8,128)} %preact_ref.1) | copy-start | bytes 6291460
  298.6 2.3 copy-start.4
  300.9 1.0 copy-start.7
  300.9 1.7 copy-start.5
  302.6 2.1 copy-start
  304.7 1.2 copy-start.1
  323.2 1.0 copy-start.3
  324.2 6.2 %copy-start.2 = (bf16[1024,512]{1,0:T(8,128)(2,1)S(1)}, bf16[1024,512]{1,0:T(8,128)(2,1)}, u32[]{:S(2)}) copy-start(bf16[1024,512]{1,0:T(8,128)(2,1)} %feat_ref.1) | copy-start | bytes 3145732
  324.2 6.3 %copy-start.6 = (bf16[1024,512]{1,0:T(8,128)(2,1)S(1)}, bf16[1024,512]{1,0:T(8,128)(2,1)}, u32[]{:S(2)}) copy-start(bf16[1024,512]{1,0:T(8,128)(2,1)} %copy-done.5) | copy-start | bytes 3145732
  326.9 22.8 %all-to-all-start.1 = ((f32[128,4,512]{2,1,0:T(4,128)}), f32[128,4,512]{2,1,0:T(4,128)S(1)}, u32[]{:S(2)}, u32[]{:S(2)}) async-start(f32[128,4,512]{2,1,0:T(4,128)} %reshape.13), calls=%async_computation.1 | async-start | bytes 2097152 | tf_op jit(solution)/shard_map/all_to_all | solution.py:162
  349.9 5.9 %copy-start.11 = (f32[512,512]{1,0:T(8,128)S(1)}, f32[512,512]{1,0:T(8,128)}, u32[]{:S(2)}) copy-start(f32[512,512]{1,0:T(8,128)} %fusion.20) | copy-start | bytes 3145732
  351.0 162.5 %all-to-all-start.2 = ((f32[128,4,512]{2,1,0:T(4,128)}), f32[128,4,512]{2,1,0:T(4,128)S(1)}, u32[]{:S(2)}, u32[]{:S(2)}) async-start(f32[128,4,512]{2,1,0:T(4,128)} %broadcast_in_dim.6), calls=%async_computation.2 | async-start | bytes 2097152 | tf_op jit(solution)/shard_map/all_to_all | solution.py:165
  355.7 155.1 %all-reduce.2.cloned.1.call-start = ((), (), s32[]{:S(2)}) async-start(), calls=%async_computation.3 | async-start | bytes 2097152 | tf_op jit(solution)/shard_map/psum | solution.py:181
Sparse Core Ops, SparseCore 0:
  361.9 148.8 all-reduce.1

commit v2 on v1

v2 whole, which is shorter than its diff:
```python
import functools
import math

import jax
import jax.numpy as jnp
from jax import lax
from jax.experimental import pallas as pl
from jax.experimental.pallas import tpu as pltpu
from jax.sharding import PartitionSpec as P

D = 512
BLK = 128
BLK_DEV = 8
OWNERS = 128
NB = 64
K = 10
COLUMNS = BLK_DEV + NB
TAG = 16
F32 = jnp.float32
BF16 = jnp.bfloat16


def dot(a, b):
    return lax.dot_general(a, b, (((1,), (0,)), ((), ())), preferred_element_type=F32)


def halves(values):
    upper = values.astype(BF16)
    return upper, (values - upper.astype(F32)).astype(BF16)


def scatter_kernel(
    col_ref, owner_ref, slot_ref, counts_ref, preact_ref, cot_ref, own_ref, send_ref, acc, stage, tags, sems, tag_sem
):
    b = pl.program_id(0)
    untagged = pltpu.make_async_copy(tags, send_ref.at[:, pl.ds(D, TAG), :], tag_sem)

    @pl.when(b == 0)
    def _():
        acc[...] = jnp.zeros_like(acc)
        tags[...] = jnp.full_like(tags, -1)
        untagged.start()

    counts = counts_ref[0].astype(F32)
    degree = 1.0 + jnp.sum(jnp.sum(counts, axis=0), axis=1, keepdims=True)
    grad = jnp.where(preact_ref[...] > 0, cot_ref[...], 0.0) / jnp.sqrt(degree)
    upper, lower = halves(grad.T)
    both = jnp.concatenate([upper, lower], axis=1)
    tiles = counts.astype(BF16)
    for t in range(0, K, 2):
        pair = jnp.concatenate([tiles[t], tiles[t + 1]], axis=1)
        part = dot(both, jnp.concatenate([pair, pair], axis=0))
        acc[col_ref[b, t]] += part[:, :BLK]
        acc[col_ref[b, t + 1]] += part[:, BLK:]

    @pl.when(b == BLK_DEV - 1)
    def _():
        own_ref[...] = acc[:BLK_DEV]
        untagged.wait()

        def put(k):
            return pltpu.make_async_copy(stage.at[k], send_ref.at[owner_ref[k]], sems.at[k])

        @pl.loop(0, NB)
        def _(k):
            stage[k, :D] = acc[BLK_DEV + k].astype(BF16)
            stage[k, D:] = jnp.full((TAG, BLK), slot_ref[k].astype(F32), F32).astype(BF16)
            put(k).start()

        @pl.loop(0, NB)
        def _(k):
            put(k).wait()


def partials(tile_col, owners, slots, counts, preact, cotangent):
    return pl.pallas_call(
        scatter_kernel,
        grid_spec=pltpu.PrefetchScalarGridSpec(
            num_scalar_prefetch=3,
            grid=(BLK_DEV,),
            in_specs=[
                pl.BlockSpec((1, K, BLK, BLK), lambda b, *_: (b, 0, 0, 0)),
                pl.BlockSpec((BLK, D), lambda b, *_: (b, 0)),
                pl.BlockSpec((BLK, D), lambda b, *_: (b, 0)),
            ],
            out_specs=[
                pl.BlockSpec((BLK_DEV, D, BLK), lambda b, *_: (0, 0, 0)),
                pl.BlockSpec(memory_space=pl.ANY),
            ],
            scratch_shapes=[
                pltpu.VMEM((COLUMNS, D, BLK), F32),
                pltpu.VMEM((NB, D + TAG, BLK), BF16),
                pltpu.VMEM((OWNERS, TAG, BLK), BF16),
                pltpu.SemaphoreType.DMA((NB,)),
                pltpu.SemaphoreType.DMA,
            ],
        ),
        out_shape=[
            jax.ShapeDtypeStruct((BLK_DEV, D, BLK), F32),
            jax.ShapeDtypeStruct((OWNERS, D + TAG, BLK), BF16),
        ],
        compiler_params=pltpu.CompilerParams(vmem_limit_bytes=56 << 20),
        cost_estimate=pl.CostEstimate(
            flops=4 * BLK_DEV * K * BLK * BLK * D, bytes_accessed=20 << 20, transcendentals=0
        ),
    )(tile_col, owners, slots, counts, preact, cotangent)


GROUP = 8


def gather_kernel(asked_ref, recv_ref, own_ref, feat_ref, total_ref, neigh_ref):
    step = pl.program_id(0)

    @pl.when(step == 0)
    def _():
        total_ref[...] = own_ref[...]

    for i in range(GROUP):
        slot = asked_ref[step * GROUP + i]

        @pl.when(slot >= 0)
        def _():
            total_ref[slot] += recv_ref[i, :D].astype(F32)

    @pl.when(step == OWNERS // GROUP - 1)
    def _():
        neigh_ref[...] = jnp.zeros_like(neigh_ref)
        for g in range(0, BLK_DEV, 2):
            upper, lower = halves(jnp.concatenate([total_ref[g], total_ref[g + 1]], axis=1))
            feat = feat_ref[g * BLK : (g + 2) * BLK, :]
            neigh_ref[...] += dot(upper, feat) + dot(lower, feat)


def whole(*shape):
    return pl.BlockSpec(shape, lambda *_: (0,) * len(shape))


def totals(asked, received, own, features):
    return pl.pallas_call(
        gather_kernel,
        grid_spec=pltpu.PrefetchScalarGridSpec(
            num_scalar_prefetch=1,
            grid=(OWNERS // GROUP,),
            in_specs=[
                pl.BlockSpec((GROUP, D + TAG, BLK), lambda s, *_: (s, 0, 0)),
                whole(BLK_DEV, D, BLK),
                whole(BLK_DEV * BLK, D),
            ],
            out_specs=[whole(BLK_DEV, D, BLK), whole(D, D)],
        ),
        out_shape=[
            jax.ShapeDtypeStruct((BLK_DEV, D, BLK), F32),
            jax.ShapeDtypeStruct((D, D), F32),
        ],
        compiler_params=pltpu.CompilerParams(vmem_limit_bytes=40 << 20),
        cost_estimate=pl.CostEstimate(
            flops=4 * BLK_DEV * BLK * D * D, bytes_accessed=20 << 20, transcendentals=0
        ),
    )(asked, received, own, features)


def feature_kernel(total_ref, base_ref, weight_ref, grad_ref):
    w_upper, w_lower = halves(weight_ref[...].T)
    upper, lower = halves(jnp.concatenate([total_ref[0], total_ref[1]], axis=1).T)
    grad_ref[...] = base_ref[...] + (dot(upper, w_upper) + dot(lower, w_upper) + dot(upper, w_lower))


def feature_gradient(total, base, weight):
    return pl.pallas_call(
        feature_kernel,
        grid=(BLK_DEV // 2,),
        in_specs=[
            pl.BlockSpec((2, D, BLK), lambda g: (g, 0, 0)),
            pl.BlockSpec((2 * BLK, D), lambda g: (g, 0)),
            whole(D, D),
        ],
        out_specs=pl.BlockSpec((2 * BLK, D), lambda g: (g, 0)),
        out_shape=jax.ShapeDtypeStruct((BLK_DEV * BLK, D), F32),
        compiler_params=pltpu.CompilerParams(vmem_limit_bytes=32 << 20),
        cost_estimate=pl.CostEstimate(
            flops=6 * BLK_DEV * BLK * D * D, bytes_accessed=7 << 20, transcendentals=0
        ),
    )(total, base, weight)


def sum_everywhere(values):
    rows = values.shape[0] // OWNERS
    shares = lax.all_to_all(values.astype(BF16).reshape(OWNERS, rows, D), "nodes", 0, 0, tiled=True)
    share = jnp.sum(shares.astype(F32), axis=0).astype(BF16)
    spread = jnp.broadcast_to(share[None], (OWNERS, rows, D))
    return lax.all_to_all(spread, "nodes", 0, 0, tiled=True).reshape(-1, D).astype(F32)


def shards(features, preact, cotangent, w_self, w_neigh, tile_counts, tile_col, owner, slot):
    own, outgoing = partials(tile_col, owner[0], slot[0], tile_counts, preact, cotangent)
    received = lax.all_to_all(outgoing, "nodes", 0, 0, tiled=True)

    grad_pre = jnp.where(preact > 0, cotangent, 0.0)
    upper, lower = halves(grad_pre)
    turned = features.T
    self_part = dot(turned, upper) + dot(turned, lower)
    w_upper, w_lower = halves(w_self.T)
    base = dot(upper, w_upper) + dot(lower, w_upper) + dot(upper, w_lower)

    asked = received[:, D, 0].astype(jnp.int32)
    total, neigh_part = totals(asked, received, own, features)
    both = sum_everywhere(jnp.concatenate([self_part, neigh_part], axis=0))
    grad_features = feature_gradient(total, base, w_neigh)
    scale = 1.0 / math.sqrt(OWNERS * BLK_DEV * BLK)
    return grad_features, both[:D] * scale, both[D:].T * scale


def solution(mesh):
    rows = P("nodes", None)
    return jax.shard_map(
        shards,
        mesh=mesh,
        in_specs=(rows, rows, rows, P(), P(), P("nodes", None, None, None), rows, rows, rows),
        out_specs=(rows, P(), P()),
        check_vma=False,
    )
```

time: 523 us -> 357 us (0.68)
  blocking collectives: 261 us -> 31.8 us
  waiting for transfers between devices: 170 us -> 250 us
  between operations: 14.2 us -> 0.82 us
  other arithmetic: 4.2 us -> 9.9 us
  local copies, waits for them, and re-layouts: 10.9 us -> 5.47 us
    all_gather x1 -> x0, blocking collectives: 261 us -> none  [shards(): lists = lax.all_gather(owner * BLK_DEV + slot, 'nodes', axis=0, tiled=True)]
    all_to_all x1, waiting for transfers between devices: 0.01 us -> 240 us  [shards(): received = lax.all_to_all(outgoing, 'nodes', 0, 0, tiled=True)]
    psum x1 -> x0, waiting for transfers between devices: 152 us -> none  [shards(): self_total = lax.psum(self_part, 'nodes')]
    all_to_all x0 -> x1, blocking collectives: none -> 31.8 us  [sum_everywhere(): lax.all_to_all(values.astype(BF16).reshape(OWNERS, rows, D), 'nodes', 0,...]
    all_to_all x2 -> x1, waiting for transfers between devices: 17.5 us -> 9.8 us  [sum_everywhere(): lax.all_to_all(spread, 'nodes', 0, 0, tiled=True).reshape(-1, D).astype(F32)]
  transfers between devices with their start and end apart: 4 -> 2, of which waited for: 2 -> 2; matrix products, arithmetic and copies ran while one was open for 3% -> 2% of each run, Pallas kernels for 0% -> 1%
where the time goes in v2:
time: 357 us; the launch traced here: 356 us
  waiting for transfers between devices  250 us (70%)
  Pallas kernels  35 us (10%)
  blocking collectives  31.8 us (9%)
  starting transfers between devices  17.5 us (5%)
  other arithmetic  9.9 us (3%)
  matrix products  5.9 us (2%)
  local copies, waits for them, and re-layouts  5.47 us (2%)
    all_to_all x1, waiting for transfers between devices, shards(): received = lax.all_to_all(outgoing, 'nodes', 0, 0, tiled=True)  240 us
    all_to_all x1, blocking collectives, sum_everywhere(): lax.all_to_all(values.astype(BF16).reshape(OWNERS, rows, D), 'nodes', 0,...  31.8 us
    pallas_call x1, Pallas kernels, partials(): pl.pallas_call(scatter_kernel, grid_spec=pltpu.PrefetchScalarGridSpec(num...  16.6 us
    pallas_call x1, Pallas kernels, totals(): pl.pallas_call(gather_kernel, grid_spec=pltpu.PrefetchScalarGridSpec(num_...  13.9 us
    all_to_all x1, starting transfers between devices, shards(): received = lax.all_to_all(outgoing, 'nodes', 0, 0, tiled=True)  11.8 us
    all_to_all x1, waiting for transfers between devices, sum_everywhere(): lax.all_to_all(spread, 'nodes', 0, 0, tiled=True).reshape(-1, D).astype(F32)  9.8 us
  transfers between devices with their start and end apart: 2, of which 2 were waited for; matrix products, arithmetic and copies ran while one was open for 2% of the time, Pallas kernels for 1%

profile of v2, /device:TPU:1, one launch (start us, length us, event | category | flops | bytes accessed | tf_op | source)
XLA Modules:
  0.0 356.1 jit_solution(17796459480102520421)
XLA Ops:
  0.6 16.6 %shard_map.112 = (f32[8,512,128]{2,1,0:T(8,128)}, bf16[128,528,128]{2,1,0:T(8,128)(2,1)}) custom-call(s32[8,10]{1,0:T(8,128)} %col_ref.1, s32[64]{0:T(128)} %bitcast.48, s32[64]{0:T(128)} %bitcast.49, s32[8,10,128,128]{3,2,1,0:T(8,128)} %counts_ref.1, f32[1024,512]{1,0:T(8,128)} %preact_ref.1, f32[1024,512]{1,0:T(8,128)} %cot_ref.1), custom_call_target="tpu_custom_call" | custom-call | flops 2684354560 | bytes 20971520 | tf_op jit(solution)/shard_map/pallas_call | solution.py:76
  17.2 0.0 copy-start.8
  17.2 11.8 %all-to-all-start = ((bf16[128,528,128]{2,1,0:T(8,128)(2,1)}), bf16[128,528,128]{2,1,0:T(8,128)(2,1)}, u32[]{:S(2)}, u32[]{:S(2)}) async-start(bf16[128,528,128]{2,1,0:T(8,128)(2,1)} %get-tuple-element.7), calls=%async_computation | async-start | bytes 34603008 | tf_op jit(solution)/shard_map/all_to_all | solution.py:197
  29.1 0.0 copy-done.8
  29.1 0.0 copy-start.1
  29.1 2.2 subtract_convert_fusion
  31.3 0.0 copy-start.4
  31.3 0.0 copy-start.6
  31.4 0.0 copy-done.1
  31.4 0.8 fusion.19
  32.1 0.2 copy-done.4
  32.3 0.3 copy-done.6
  32.7 1.6 fusion.1
  34.2 239.9 %all-to-all-done.recv_ref = bf16[128,528,128]{2,1,0:T(8,128)(2,1)} async-done(((bf16[128,528,128]{2,1,0:T(8,128)(2,1)}), bf16[128,528,128]{2,1,0:T(8,128)(2,1)}, u32[]{:S(2)}, u32[]{:S(2)}) %all-to-all-start) | async-done | bytes 17301536 | tf_op jit(solution)/shard_map/all_to_all | solution.py:197
  274.2 3.3 fusion.7.asked_ref
  277.5 0.0 copy-start
  277.5 1.6 copy-done
  279.1 0.0 copy-start.9
  279.1 13.9 %shard_map.113 = (f32[8,512,128]{2,1,0:T(8,128)S(1)}, f32[512,512]{1,0:T(8,128)S(1)}) custom-call(s32[128]{0:T(128)S(1)} %fusion.7.asked_ref, bf16[128,528,128]{2,1,0:T(8,128)(2,1)} %all-to-all-done.recv_ref, f32[8,512,128]{2,1,0:T(8,128)S(1)} %copy-done, bf16[1024,512]{1,0:T(8,128)(2,1)S(1)} %copy-done.1), custom_call_target="tpu_custom_call" | custom-call | flops 1073741824 | bytes 20971520 | tf_op jit(solution)/shard_map/pallas_call | solution.py:140
  293.0 0.1 convert.10
  293.0 0.0 copy-done.9
  293.1 0.1 maximum_bitcast_fusion
  293.1 31.8 %all_to_all.15 = bf16[128,8,512]{2,1,0:T(8,128)(2,1)} all-to-all(bf16[128,8,512]{2,1,0:T(8,128)(2,1)S(1)} %maximum_bitcast_fusion), channel_id=1, replica_groups=mesh['nodes'=128] {'nodes'}, dimensions={0} | all-to-all | bytes 2097152 | tf_op jit(solution)/shard_map/all_to_all | solution.py:189
  324.9 0.0 copy-start.3
  324.9 1.5 reduce_sum.12
  326.4 1.1 broadcast_in_dim.4
  327.5 5.7 %all-to-all-start.2 = ((bf16[128,8,512]{2,1,0:T(8,128)(2,1)}), bf16[128,8,512]{2,1,0:T(8,128)(2,1)}, u32[]{:S(2)}, u32[]{:S(2)}) async-start(bf16[128,8,512]{2,1,0:T(8,128)(2,1)} %broadcast_in_dim.4), calls=%async_computation.2 | async-start | bytes 2097152 | tf_op jit(solution)/shard_map/all_to_all | solution.py:192
  333.2 0.0 copy-done.3
  333.2 0.0 copy-start.7
  333.2 2.1 fusion.13
  335.3 0.0 copy-done.7
  335.3 0.0 copy-start.5
  335.3 0.7 fusion.15
  336.0 0.5 copy-done.5
  336.5 0.0 copy-start.2
  336.5 0.7 add_add_fusion.base_ref
  337.3 0.5 copy-done.2
  337.7 4.5 %shard_map.114 = f32[1024,512]{1,0:T(8,128)} custom-call(f32[8,512,128]{2,1,0:T(8,128)S(1)} %get-tuple-element.9.total_ref, f32[1024,512]{1,0:T(8,128)S(1)} %add_add_fusion.base_ref, f32[512,512]{1,0:T(8,128)S(1)} %copy-done.2), custom_call_target="tpu_custom_call" | custom-call | flops 1610612736 | bytes 7340032 | tf_op jit(solution)/shard_map/pallas_call | solution.py:170
  342.2 9.8 %all-to-all-done.2 = bf16[128,8,512]{2,1,0:T(8,128)(2,1)} async-done(((bf16[128,8,512]{2,1,0:T(8,128)(2,1)}), bf16[128,8,512]{2,1,0:T(8,128)(2,1)}, u32[]{:S(2)}, u32[]{:S(2)}) %all-to-all-start.2) | async-done | bytes 1048608 | tf_op jit(solution)/shard_map/all_to_all | solution.py:192
  352.0 1.5 convert_element_type.43
  353.5 1.2 fusion.2
  354.8 1.3 copy.13
Async XLA Ops:
  17.2 11.9 %copy-start.8 = (f32[1024,512]{1,0:T(8,128)S(1)}, f32[1024,512]{1,0:T(8,128)}, u32[]{:S(2)}) copy-start(f32[1024,512]{1,0:T(8,128)} %preact_ref.1) | copy-start | bytes 6291460
  17.2 256.9 %all-to-all-start = ((bf16[128,528,128]{2,1,0:T(8,128)(2,1)}), bf16[128,528,128]{2,1,0:T(8,128)(2,1)}, u32[]{:S(2)}, u32[]{:S(2)}) async-start(bf16[128,528,128]{2,1,0:T(8,128)(2,1)} %get-tuple-element.7), calls=%async_computation | async-start | bytes 34603008 | tf_op jit(solution)/shard_map/all_to_all | solution.py:197
  29.1 2.3 copy-start.1
  31.3 1.0 copy-start.4
  31.3 1.3 copy-start.6
  277.5 1.6 copy-start
  279.1 14.0 %copy-start.9 = (bf16[512,512]{1,0:T(8,128)(2,1)S(1)}, bf16[512,512]{1,0:T(8,128)(2,1)}, u32[]{:S(2)}) copy-start(bf16[512,512]{1,0:T(8,128)(2,1)} %fusion.1) | copy-start | bytes 1572868
  324.9 8.3 %copy-start.3 = (f32[512,512]{1,0:T(8,128)S(1)}, f32[512,512]{1,0:T(8,128)}, u32[]{:S(2)}) copy-start(f32[512,512]{1,0:T(8,128)} %param.12) | copy-start | bytes 3145732
  327.5 24.5 %all-to-all-start.2 = ((bf16[128,8,512]{2,1,0:T(8,128)(2,1)}), bf16[128,8,512]{2,1,0:T(8,128)(2,1)}, u32[]{:S(2)}, u32[]{:S(2)}) async-start(bf16[128,8,512]{2,1,0:T(8,128)(2,1)} %broadcast_in_dim.4), calls=%async_computation.2 | async-start | bytes 2097152 | tf_op jit(solution)/shard_map/all_to_all | solution.py:192
  333.2 2.1 copy-start.7
  335.3 1.2 copy-start.5
  336.5 1.2 copy-start.2

commit v3 on v2

--- a/solution.py
+++ b/solution.py
@@ -194,14 +194,16 @@
 
 def shards(features, preact, cotangent, w_self, w_neigh, tile_counts, tile_col, owner, slot):
     own, outgoing = partials(tile_col, owner[0], slot[0], tile_counts, preact, cotangent)
-    received = lax.all_to_all(outgoing, "nodes", 0, 0, tiled=True)
-
     grad_pre = jnp.where(preact > 0, cotangent, 0.0)
     upper, lower = halves(grad_pre)
     turned = features.T
     self_part = dot(turned, upper) + dot(turned, lower)
     w_upper, w_lower = halves(w_self.T)
     base = dot(upper, w_upper) + dot(lower, w_upper) + dot(upper, w_lower)
+
+    outgoing, self_part, base = lax.optimization_barrier((outgoing, self_part, base))
+    received = lax.all_to_all(outgoing, "nodes", 0, 0, tiled=True)
+    received, self_part, base = lax.optimization_barrier((received, self_part, base))
 
     asked = received[:, D, 0].astype(jnp.int32)
     total, neigh_part = totals(asked, received, own, features)

time: 357 us -> 318 us (0.89)
  waiting for transfers between devices: 250 us -> 12.8 us
  blocking collectives: 31.8 us -> 239 us
  starting transfers between devices: 17.5 us -> 5.64 us
  local copies, waits for them, and re-layouts: 5.47 us -> 9.27 us
    all_to_all x1 -> x0, waiting for transfers between devices: 240 us -> none  [shards(): received = lax.all_to_all(outgoing, 'nodes', 0, 0, tiled=True)]
    all_to_all x0 -> x1, blocking collectives: none -> 212 us  [shards(): received = lax.all_to_all(outgoing, 'nodes', 0, 0, tiled=True)]
    all_to_all x1 -> x0, starting transfers between devices: 11.8 us -> none  [shards(): received = lax.all_to_all(outgoing, 'nodes', 0, 0, tiled=True)]
    all_to_all x1, blocking collectives: 31.8 us -> 27.2 us  [sum_everywhere(): lax.all_to_all(values.astype(BF16).reshape(OWNERS, rows, D), 'nodes', 0,...]
    unnamed x21 -> x17, local copies, waits for them, and re-layouts: 4.39 us -> 8.23 us
  transfers between devices with their start and end apart: 2 -> 1, of which waited for: 2 -> 1; matrix products, arithmetic and copies ran while one was open for 2% -> 0% of each run, Pallas kernels for 1% -> 1%
where the time goes in v3:
time: 318 us; the launch traced here: 317 us
  blocking collectives  239 us (75%)
  Pallas kernels  34.9 us (11%)
  waiting for transfers between devices  12.8 us (4%)
  other arithmetic  9.59 us (3%)
  local copies, waits for them, and re-layouts  9.27 us (3%)
  starting transfers between devices  5.64 us (2%)
  matrix products  4.64 us (1%)
    all_to_all x1, blocking collectives, shards(): received = lax.all_to_all(outgoing, 'nodes', 0, 0, tiled=True)  212 us
    all_to_all x1, blocking collectives, sum_everywhere(): lax.all_to_all(values.astype(BF16).reshape(OWNERS, rows, D), 'nodes', 0,...  27.2 us
    pallas_call x1, Pallas kernels, partials(): pl.pallas_call(scatter_kernel, grid_spec=pltpu.PrefetchScalarGridSpec(num...  16.5 us
    pallas_call x1, Pallas kernels, totals(): pl.pallas_call(gather_kernel, grid_spec=pltpu.PrefetchScalarGridSpec(num_...  14 us
    all_to_all x1, waiting for transfers between devices, sum_everywhere(): lax.all_to_all(spread, 'nodes', 0, 0, tiled=True).reshape(-1, D).astype(F32)  12.8 us
    unnamed x17, local copies, waits for them, and re-layouts  8.23 us
  transfers between devices with their start and end apart: 1, of which 1 were waited for; matrix products, arithmetic and copies ran while one was open for 0% of the time, Pallas kernels for 1%

profile of v3, /device:TPU:1, one launch (start us, length us, event | category | flops | bytes accessed | tf_op | source)
XLA Modules:
  0.0 316.8 jit_solution(9844549319853219093)
XLA Ops:
  0.6 0.0 copy-start.3
  0.6 2.9 subtract_convert_fusion
  3.5 0.0 copy-done.3
  3.5 0.0 copy-start.6
  3.5 0.8 fusion.17
  4.3 0.4 copy-done.6
  4.7 0.7 fusion.11
  5.5 0.7 fusion.13
  6.2 1.6 fusion
  7.8 0.8 add_add_fusion.base_ref
  8.6 16.5 %shard_map.112 = (f32[8,512,128]{2,1,0:T(8,128)}, bf16[128,528,128]{2,1,0:T(8,128)(2,1)}) custom-call(s32[8,10]{1,0:T(8,128)} %col_ref.1, s32[64]{0:T(128)} %bitcast.48, s32[64]{0:T(128)} %bitcast.49, s32[8,10,128,128]{3,2,1,0:T(8,128)} %counts_ref.1, f32[1024,512]{1,0:T(8,128)} %preact_ref.1, f32[1024,512]{1,0:T(8,128)} %cot_ref.1), custom_call_target="tpu_custom_call" | custom-call | flops 2684354560 | bytes 20971520 | tf_op jit(solution)/shard_map/pallas_call | solution.py:76
  25.1 0.0 copy-start.2
  25.1 212.0 %all_to_all.15.recv_ref = bf16[128,528,128]{2,1,0:T(8,128)(2,1)S(1)} all-to-all(bf16[128,528,128]{2,1,0:T(8,128)(2,1)} %get-tuple-element.14), channel_id=1, replica_groups=mesh['nodes'=128] {'nodes'}, dimensions={0} | all-to-all | bytes 34603008 | tf_op jit(solution)/shard_map/all_to_all | solution.py:205
  237.1 0.0 copy-start.5
  237.1 2.4 convert_reduce_fusion.asked_ref
  239.5 3.6 %copy-done.5 = bf16[128,528,128]{2,1,0:T(8,128)(2,1)} copy-done((bf16[128,528,128]{2,1,0:T(8,128)(2,1)}, bf16[128,528,128]{2,1,0:T(8,128)(2,1)S(1)}, u32[]{:S(2)}) %copy-start.5) | copy-done | bytes 17301528
  243.1 0.0 copy-done.2
  243.1 0.0 copy-start.7
  243.1 14.0 %shard_map.113 = (f32[8,512,128]{2,1,0:T(8,128)S(1)}, f32[512,512]{1,0:T(8,128)S(1)}) custom-call(s32[128]{0:T(128)S(1)} %convert_reduce_fusion.asked_ref, bf16[128,528,128]{2,1,0:T(8,128)(2,1)} %copy-done.5, f32[8,512,128]{2,1,0:T(8,128)S(1)} %copy-done.2, bf16[1024,512]{1,0:T(8,128)(2,1)S(1)} %copy-done.3), custom_call_target="tpu_custom_call" | custom-call | flops 1073741824 | bytes 20971520 | tf_op jit(solution)/shard_map/pallas_call | solution.py:140
  257.0 0.0 copy-start
  257.0 1.3 copy-done
  258.3 0.1 convert.9
  258.4 0.0 copy-done.7
  258.4 0.1 maximum_bitcast_fusion
  258.5 27.2 %all_to_all.16 = bf16[128,8,512]{2,1,0:T(8,128)(2,1)} all-to-all(bf16[128,8,512]{2,1,0:T(8,128)(2,1)S(1)} %maximum_bitcast_fusion), channel_id=1, replica_groups=mesh['nodes'=128] {'nodes'}, dimensions={0} | all-to-all | bytes 2097152 | tf_op jit(solution)/shard_map/all_to_all | solution.py:189
  285.7 0.0 copy-start.4
  285.7 1.5 reduce_sum.12
  287.2 1.0 broadcast_in_dim.4
  288.3 5.6 %all-to-all-start.2 = ((bf16[128,8,512]{2,1,0:T(8,128)(2,1)}), bf16[128,8,512]{2,1,0:T(8,128)(2,1)}, u32[]{:S(2)}, u32[]{:S(2)}) async-start(bf16[128,8,512]{2,1,0:T(8,128)(2,1)} %broadcast_in_dim.4), calls=%async_computation.2 | async-start | bytes 2097152 | tf_op jit(solution)/shard_map/all_to_all | solution.py:192
  293.9 0.0 copy-done.4
  293.9 0.0 copy-start.1
  294.0 1.6 copy-done.1
  295.5 4.5 %shard_map.114 = f32[1024,512]{1,0:T(8,128)} custom-call(f32[8,512,128]{2,1,0:T(8,128)S(1)} %copy-done.1, f32[1024,512]{1,0:T(8,128)S(1)} %add_add_fusion.base_ref, f32[512,512]{1,0:T(8,128)S(1)} %copy-done.4), custom_call_target="tpu_custom_call" | custom-call | flops 1610612736 | bytes 7340032 | tf_op jit(solution)/shard_map/pallas_call | solution.py:170
  300.0 12.8 %all-to-all-done.2 = bf16[128,8,512]{2,1,0:T(8,128)(2,1)} async-done(((bf16[128,8,512]{2,1,0:T(8,128)(2,1)}), bf16[128,8,512]{2,1,0:T(8,128)(2,1)}, u32[]{:S(2)}, u32[]{:S(2)}) %all-to-all-start.2) | async-done | bytes 1048608 | tf_op jit(solution)/shard_map/all_to_all | solution.py:192
  312.8 1.5 convert_element_type.43
  314.3 1.2 fusion.1
  315.5 1.3 copy.17
Async XLA Ops:
  0.6 2.9 copy-start.3
  3.5 1.2 copy-start.6
  25.1 218.0 %copy-start.2 = (f32[8,512,128]{2,1,0:T(8,128)S(1)}, f32[8,512,128]{2,1,0:T(8,128)}, u32[]{:S(2)}) copy-start(f32[8,512,128]{2,1,0:T(8,128)} %get-tuple-element.18.own_ref) | copy-start | bytes 6291460
  237.1 5.9 %copy-start.5 = (bf16[128,528,128]{2,1,0:T(8,128)(2,1)}, bf16[128,528,128]{2,1,0:T(8,128)(2,1)S(1)}, u32[]{:S(2)}) copy-start(bf16[128,528,128]{2,1,0:T(8,128)(2,1)S(1)} %all_to_all.15.recv_ref) | copy-start | bytes 51904516
  243.1 15.4 %copy-start.7 = (bf16[512,512]{1,0:T(8,128)(2,1)S(1)}, bf16[512,512]{1,0:T(8,128)(2,1)}, u32[]{:S(2)}) copy-start(bf16[512,512]{1,0:T(8,128)(2,1)} %fusion) | copy-start | bytes 1572868
  257.0 1.3 copy-start
  285.7 8.2 %copy-start.4 = (f32[512,512]{1,0:T(8,128)S(1)}, f32[512,512]{1,0:T(8,128)}, u32[]{:S(2)}) copy-start(f32[512,512]{1,0:T(8,128)} %weight_ref.1) | copy-start | bytes 3145732
  288.3 24.5 %all-to-all-start.2 = ((bf16[128,8,512]{2,1,0:T(8,128)(2,1)}), bf16[128,8,512]{2,1,0:T(8,128)(2,1)}, u32[]{:S(2)}, u32[]{:S(2)}) async-start(bf16[128,8,512]{2,1,0:T(8,128)(2,1)} %broadcast_in_dim.4), calls=%async_computation.2 | async-start | bytes 2097152 | tf_op jit(solution)/shard_map/all_to_all | solution.py:192
  293.9 1.6 copy-start.1

commit v4 on v2

v4 whole, which is shorter than its diff:
```python
import functools
import math

import jax
import jax.numpy as jnp
from jax import lax
from jax.experimental import pallas as pl
from jax.experimental.pallas import tpu as pltpu
from jax.sharding import PartitionSpec as P

D = 512
BLK = 128
BLK_DEV = 8
OWNERS = 128
NB = 64
K = 10
COLUMNS = BLK_DEV + NB
TAG = 16
F32 = jnp.float32
BF16 = jnp.bfloat16


def dot(a, b):
    return lax.dot_general(a, b, (((1,), (0,)), ((), ())), preferred_element_type=F32)


def halves(values):
    upper = values.astype(BF16)
    return upper, (values - upper.astype(F32)).astype(BF16)


def whole(*shape):
    return pl.BlockSpec(shape, lambda *_: (0,) * len(shape))


def scatter_kernel(
    col_ref,
    owner_ref,
    slot_ref,
    counts_ref,
    preact_ref,
    cot_ref,
    feat_ref,
    own_ref,
    self_ref,
    send_ref,
    acc,
    stage,
    tags,
    sems,
    tag_sem,
):
    b = pl.program_id(0)
    untagged = pltpu.make_async_copy(tags, send_ref.at[:, pl.ds(D, TAG), :], tag_sem)

    @pl.when(b == 0)
    def _():
        acc[...] = jnp.zeros_like(acc)
        self_ref[...] = jnp.zeros_like(self_ref)
        tags[...] = jnp.full_like(tags, -1)
        untagged.start()

    counts = counts_ref[0].astype(F32)
    degree = 1.0 + jnp.sum(jnp.sum(counts, axis=0), axis=1, keepdims=True)
    root = jnp.broadcast_to(jnp.sqrt(degree), (BLK, BLK)).T[:1]
    grad = jnp.where(preact_ref[...] > 0, cot_ref[...], 0.0).T
    both = jnp.concatenate(halves(grad), axis=1)
    feat = feat_ref[...]
    self_ref[...] += dot(both, jnp.concatenate([feat, feat], axis=0))
    both = jnp.concatenate(halves(grad / root), axis=1)
    tiles = counts.astype(BF16)
    for t in range(0, K, 2):
        pair = jnp.concatenate([tiles[t], tiles[t + 1]], axis=1)
        part = dot(both, jnp.concatenate([pair, pair], axis=0))
        acc[col_ref[b, t]] += part[:, :BLK]
        acc[col_ref[b, t + 1]] += part[:, BLK:]

    @pl.when(b == BLK_DEV - 1)
    def _():
        untagged.wait()

        def put(k):
            return pltpu.make_async_copy(stage.at[k], send_ref.at[owner_ref[k]], sems.at[k])

        @pl.loop(0, NB)
        def _(k):
            stage[k, :D] = acc[BLK_DEV + k].astype(BF16)
            stage[k, D:] = jnp.full((TAG, BLK), slot_ref[k].astype(F32), F32).astype(BF16)
            put(k).start()

        own_ref[...] = acc[:BLK_DEV]
        self_ref[...] = self_ref[...].T

        @pl.loop(0, NB)
        def _(k):
            put(k).wait()


def partials(tile_col, owners, slots, counts, preact, cotangent, features):
    rows = pl.BlockSpec((BLK, D), lambda b, *_: (b, 0))
    return pl.pallas_call(
        scatter_kernel,
        grid_spec=pltpu.PrefetchScalarGridSpec(
            num_scalar_prefetch=3,
            grid=(BLK_DEV,),
            in_specs=[pl.BlockSpec((1, K, BLK, BLK), lambda b, *_: (b, 0, 0, 0)), rows, rows, rows],
            out_specs=[whole(BLK_DEV, D, BLK), whole(D, D), pl.BlockSpec(memory_space=pl.ANY)],
            scratch_shapes=[
                pltpu.VMEM((COLUMNS, D, BLK), F32),
                pltpu.VMEM((NB, D + TAG, BLK), BF16),
                pltpu.VMEM((OWNERS, TAG, BLK), BF16),
                pltpu.SemaphoreType.DMA((NB,)),
                pltpu.SemaphoreType.DMA,
            ],
        ),
        out_shape=[
            jax.ShapeDtypeStruct((BLK_DEV, D, BLK), F32),
            jax.ShapeDtypeStruct((D, D), F32),
            jax.ShapeDtypeStruct((OWNERS, D + TAG, BLK), BF16),
        ],
        compiler_params=pltpu.CompilerParams(vmem_limit_bytes=58 << 20),
        cost_estimate=pl.CostEstimate(
            flops=4 * BLK_DEV * K * BLK * BLK * D, bytes_accessed=22 << 20, transcendentals=0
        ),
    )(tile_col, owners, slots, counts, preact, cotangent, features)


GROUP = 8
STEPS = OWNERS // GROUP
SHARE = BLK_DEV * D // STEPS


def gather_kernel(asked_ref, recv_ref, own_ref, feat_ref, self_ref, total_ref, joined_ref):
    step = pl.program_id(0)

    @pl.when(step == 0)
    def _():
        total_ref[...] = jnp.zeros_like(total_ref)

    for i in range(GROUP):
        slot = asked_ref[step * GROUP + i]

        @pl.when(slot >= 0)
        def _():
            total_ref[slot] += recv_ref[i, :D].astype(F32)

    share = pl.ds(pl.multiple_of(step % (D // SHARE) * SHARE, SHARE), SHARE)
    total_ref[step // (D // SHARE), share] += own_ref[0]

    @pl.when(step == STEPS - 1)
    def _():
        neigh = jnp.zeros((D, D), F32)
        for g in range(0, BLK_DEV, 2):
            upper, lower = halves(jnp.concatenate([total_ref[g], total_ref[g + 1]], axis=1))
            feat = feat_ref[g * BLK : (g + 2) * BLK, :]
            neigh += dot(upper, feat) + dot(lower, feat)
        joined_ref[:D] = self_ref[...].astype(BF16)
        joined_ref[D:] = neigh.T.astype(BF16)


def totals(asked, received, own, features, self_part):
    return pl.pallas_call(
        gather_kernel,
        grid_spec=pltpu.PrefetchScalarGridSpec(
            num_scalar_prefetch=1,
            grid=(STEPS,),
            in_specs=[
                pl.BlockSpec((GROUP, D + TAG, BLK), lambda s, *_: (s, 0, 0)),
                pl.BlockSpec((1, SHARE, BLK), lambda s, *_: (s, 0, 0)),
                whole(BLK_DEV * BLK, D),
                whole(D, D),
            ],
            out_specs=[whole(BLK_DEV, D, BLK), whole(2 * D, D)],
        ),
        out_shape=[
            jax.ShapeDtypeStruct((BLK_DEV, D, BLK), F32),
            jax.ShapeDtypeStruct((2 * D, D), BF16),
        ],
        compiler_params=pltpu.CompilerParams(vmem_limit_bytes=20 << 20),
        cost_estimate=pl.CostEstimate(
            flops=4 * BLK_DEV * BLK * D * D, bytes_accessed=20 << 20, transcendentals=0
        ),
    )(asked, received, own.reshape(STEPS, SHARE, BLK), features, self_part)


def feature_kernel(total_ref, preact_ref, cot_ref, self_ref, neigh_ref, grad_ref):
    grad = jnp.where(preact_ref[...] > 0, cot_ref[...], 0.0)
    upper, lower = halves(grad)
    w_upper, w_lower = halves(self_ref[...].T)
    result = dot(upper, w_upper) + dot(lower, w_upper) + dot(upper, w_lower)
    upper, lower = halves(jnp.concatenate([total_ref[0], total_ref[1]], axis=1).T)
    w_upper, w_lower = halves(neigh_ref[...].T)
    grad_ref[...] = result + (dot(upper, w_upper) + dot(lower, w_upper) + dot(upper, w_lower))


def feature_gradient(total, preact, cotangent, w_self, w_neigh):
    rows = pl.BlockSpec((2 * BLK, D), lambda g: (g, 0))
    return pl.pallas_call(
        feature_kernel,
        grid=(BLK_DEV // 2,),
        in_specs=[pl.BlockSpec((2, D, BLK), lambda g: (g, 0, 0)), rows, rows, whole(D, D), whole(D, D)],
        out_specs=rows,
        out_shape=jax.ShapeDtypeStruct((BLK_DEV * BLK, D), F32),
        compiler_params=pltpu.CompilerParams(vmem_limit_bytes=16 << 20),
        cost_estimate=pl.CostEstimate(
            flops=12 * BLK_DEV * BLK * D * D, bytes_accessed=10 << 20, transcendentals=0
        ),
    )(total, preact, cotangent, w_self, w_neigh)


def shards(features, preact, cotangent, w_self, w_neigh, tile_counts, tile_col, owner, slot):
    own, self_part, outgoing = partials(tile_col, owner[0], slot[0], tile_counts, preact, cotangent, features)
    received = lax.all_to_all(outgoing, "nodes", 0, 0, tiled=True)
    asked = received[:, D, 0].astype(jnp.int32)
    total, joined = totals(asked, received, own, features, self_part)

    rows = 2 * D // OWNERS
    shares = lax.all_to_all(joined.reshape(OWNERS, rows, D), "nodes", 0, 0, tiled=True)
    share = jnp.sum(shares.astype(F32), axis=0).astype(BF16)
    share, total = lax.optimization_barrier((share, total))
    spread = jnp.broadcast_to(share[None], (OWNERS, rows, D))
    both = lax.all_to_all(spread, "nodes", 0, 0, tiled=True).reshape(2 * D, D)
    grad_features = feature_gradient(total, preact, cotangent, w_self, w_neigh)
    scale = 1.0 / math.sqrt(OWNERS * BLK_DEV * BLK)
    return grad_features, both[:D].astype(F32) * scale, both[D:].astype(F32) * scale


def solution(mesh):
    rows = P("nodes", None)
    return jax.shard_map(
        shards,
        mesh=mesh,
        in_specs=(rows, rows, rows, P(), P(), P("nodes", None, None, None), rows, rows, rows),
        out_specs=(rows, P(), P()),
        check_vma=False,
    )
```

time: 357 us -> 297 us (0.83)
  waiting for transfers between devices: 250 us -> 8.6 us
  blocking collectives: 31.8 us -> 239 us
  starting transfers between devices: 17.5 us -> 5.64 us
  Pallas kernels: 35 us -> 28.5 us
  matrix products: 5.9 us -> 0 us
    all_to_all x2 -> x1, waiting for transfers between devices: 250 us -> 8.6 us  [shards(): both = lax.all_to_all(spread, 'nodes', 0, 0, tiled=True).reshape(2 * D, D)]
    all_to_all x1 -> x2, blocking collectives: 31.8 us -> 239 us  [the longest x1 212 us: shards(): received = lax.all_to_all(outgoing, 'nodes', 0, 0, tiled=True)]
    all_to_all x2 -> x1, starting transfers between devices: 17.5 us -> 5.64 us  [shards(): both = lax.all_to_all(spread, 'nodes', 0, 0, tiled=True).reshape(2 * D, D)]
    pallas_call x1, Pallas kernels: 13.9 us -> 5.18 us  [totals(): pl.pallas_call(gather_kernel, grid_spec=pltpu.PrefetchScalarGridSpec(num_...]
    dot_general x5 -> x0, matrix products: 5.9 us -> none  [dot(): lax.dot_general(a, b, (((1,), (0,)), ((), ())), preferred_element_type=F32)]
    convert_element_type x3 -> x0, other arithmetic: 3.79 us -> none  [the longest x1 2.22 us: halves(): return (upper, (values - upper.astype(F32)).astype(BF16))]
  transfers between devices with their start and end apart: 2 -> 1, of which waited for: 2 -> 1; matrix products, arithmetic and copies ran while one was open for 2% -> 0% of each run, Pallas kernels for 1% -> 2%
where the time goes in v4:
time: 297 us; the launch traced here: 296 us
  blocking collectives  239 us (80%)
  Pallas kernels  28.5 us (10%)
  waiting for transfers between devices  8.6 us (3%)
  local copies, waits for them, and re-layouts  6.78 us (2%)
  other arithmetic  6.73 us (2%)
  starting transfers between devices  5.64 us (2%)
    all_to_all x1, blocking collectives, shards(): received = lax.all_to_all(outgoing, 'nodes', 0, 0, tiled=True)  212 us
    all_to_all x1, blocking collectives, shards(): lax.all_to_all(joined.reshape(OWNERS, rows, D), 'nodes', 0, 0, tiled=True)  27.2 us
    pallas_call x1, Pallas kernels, partials(): pl.pallas_call(scatter_kernel, grid_spec=pltpu.PrefetchScalarGridSpec(num...  17.5 us
    all_to_all x1, waiting for transfers between devices, shards(): both = lax.all_to_all(spread, 'nodes', 0, 0, tiled=True).reshape(2 * D, D)  8.6 us
  transfers between devices with their start and end apart: 1, of which 1 were waited for; matrix products, arithmetic and copies ran while one was open for 0% of the time, Pallas kernels for 2%

profile of v4, /device:TPU:1, one launch (start us, length us, event | category | flops | bytes accessed | tf_op | source)
XLA Modules:
  0.0 296.2 jit_solution(16618050423752194989)
XLA Ops:
  0.6 17.5 %shard_map.112 = (f32[8,512,128]{2,1,0:T(8,128)}, f32[512,512]{1,0:T(8,128)}, bf16[128,528,128]{2,1,0:T(8,128)(2,1)}) custom-call(s32[8,10]{1,0:T(8,128)} %col_ref.1, s32[64]{0:T(128)} %bitcast.10, s32[64]{0:T(128)} %bitcast.11, s32[8,10,128,128]{3,2,1,0:T(8,128)} %counts_ref.1, f32[1024,512]{1,0:T(8,128)} %preact_ref.3, f32[1024,512]{1,0:T(8,128)} %cot_ref.3, ...), custom_call_target="tpu_custom_call" | custom-call | flops 2684354560 | bytes 23068672 | tf_op jit(solution)/shard_map/pallas_call | solution.py:101
  18.1 0.0 copy-start
  18.2 0.0 copy-start.3
  18.2 0.0 copy-start.4
  18.2 212.0 %all_to_all.15.recv_ref = bf16[128,528,128]{2,1,0:T(8,128)(2,1)S(1)} all-to-all(bf16[128,528,128]{2,1,0:T(8,128)(2,1)} %get-tuple-element.10), channel_id=1, replica_groups=mesh['nodes'=128] {'nodes'}, dimensions={0} | all-to-all | bytes 34603008 | tf_op jit(solution)/shard_map/all_to_all | solution.py:213
  230.2 2.4 fusion.asked_ref
  232.5 0.0 copy-done
  232.5 0.0 copy-done.3
  232.5 0.0 copy-done.4
  232.6 5.2 %shard_map.113 = (f32[8,512,128]{2,1,0:T(8,128)S(1)}, bf16[1024,512]{1,0:T(8,128)(2,1)S(1)}) custom-call(s32[128]{0:T(128)S(1)} %fusion.asked_ref, bf16[128,528,128]{2,1,0:T(8,128)(2,1)S(1)} %all_to_all.15.recv_ref, f32[16,256,128]{2,1,0:T(8,128)S(1)} %bitcast.8, bf16[1024,512]{1,0:T(8,128)(2,1)S(1)} %copy-done, f32[512,512]{1,0:T(8,128)S(1)} %copy-done.4), custom_call_target="tpu_custom_call" | custom-call | flops 1073741824 | bytes 20971520 | tf_op jit(solution)/shard_map/pallas_call | solution.py:162
  237.7 0.0 copy-start.5
  237.8 1.3 copy-done.5
  239.1 27.2 %all_to_all.16 = bf16[128,8,512]{2,1,0:T(8,128)(2,1)} all-to-all(bf16[128,8,512]{2,1,0:T(8,128)(2,1)S(1)} %bitcast.9), channel_id=1, replica_groups=mesh['nodes'=128] {'nodes'}, dimensions={0} | all-to-all | bytes 2097152 | tf_op jit(solution)/shard_map/all_to_all | solution.py:218
  266.3 0.0 copy-start.1
  266.3 0.0 copy-start.7
  266.3 1.6 reduce_sum.12
  267.9 1.0 broadcast_in_dim.2
  268.9 5.6 %all-to-all-start.2 = ((bf16[128,8,512]{2,1,0:T(8,128)(2,1)}), bf16[128,8,512]{2,1,0:T(8,128)(2,1)}, u32[]{:S(2)}, u32[]{:S(2)}) async-start(bf16[128,8,512]{2,1,0:T(8,128)(2,1)} %broadcast_in_dim.2), calls=%async_computation.2 | async-start | bytes 2097152 | tf_op jit(solution)/shard_map/all_to_all | solution.py:222
  274.6 0.0 copy-done.1
  274.6 0.0 copy-done.7
  274.6 0.0 copy-start.2
  274.6 1.6 copy-done.2
  276.2 0.0 copy-start.6
  276.2 1.6 copy-done.6
  277.8 0.0 copy-start.8
  277.8 1.2 copy-done.8
  279.0 5.8 %shard_map.114 = f32[1024,512]{1,0:T(8,128)} custom-call(f32[8,512,128]{2,1,0:T(8,128)S(1)} %copy-done.6, f32[1024,512]{1,0:T(8,128)S(1)} %copy-done.1, f32[1024,512]{1,0:T(8,128)S(1)} %copy-done.2, f32[512,512]{1,0:T(8,128)S(1)} %copy-done.7, f32[512,512]{1,0:T(8,128)S(1)} %copy-done.8), custom_call_target="tpu_custom_call" | custom-call | flops 3221225472 | bytes 10485760 | tf_op jit(solution)/shard_map/pallas_call | solution.py:198
  284.8 8.6 %all-to-all-done.2 = bf16[128,8,512]{2,1,0:T(8,128)(2,1)} async-done(((bf16[128,8,512]{2,1,0:T(8,128)(2,1)}), bf16[128,8,512]{2,1,0:T(8,128)(2,1)}, u32[]{:S(2)}, u32[]{:S(2)}) %all-to-all-start.2) | async-done | bytes 1048608 | tf_op jit(solution)/shard_map/all_to_all | solution.py:222
  293.4 2.8 multiply_bitcast_fusion
Async XLA Ops:
  18.1 214.4 %copy-start = (bf16[1024,512]{1,0:T(8,128)(2,1)S(1)}, bf16[1024,512]{1,0:T(8,128)(2,1)}, u32[]{:S(2)}) copy-start(bf16[1024,512]{1,0:T(8,128)(2,1)} %feat_ref.3) | copy-start | bytes 3145732
  18.2 214.4 %copy-start.3 = (f32[8,512,128]{2,1,0:T(8,128)S(1)}, f32[8,512,128]{2,1,0:T(8,128)}, u32[]{:S(2)}) copy-start(f32[8,512,128]{2,1,0:T(8,128)} %get-tuple-element.11) | copy-start | bytes 6291460
  18.2 214.4 %copy-start.4 = (f32[512,512]{1,0:T(8,128)S(1)}, f32[512,512]{1,0:T(8,128)}, u32[]{:S(2)}) copy-start(f32[512,512]{1,0:T(8,128)} %get-tuple-element.12.self_ref) | copy-start | bytes 3145732
  237.7 1.3 copy-start.5
  266.3 8.3 %copy-start.1 = (f32[1024,512]{1,0:T(8,128)S(1)}, f32[1024,512]{1,0:T(8,128)}, u32[]{:S(2)}) copy-start(f32[1024,512]{1,0:T(8,128)} %preact_ref.3) | copy-start | bytes 6291460
  266.3 8.3 %copy-start.7 = (f32[512,512]{1,0:T(8,128)S(1)}, f32[512,512]{1,0:T(8,128)}, u32[]{:S(2)}) copy-start(f32[512,512]{1,0:T(8,128)} %self_ref.1) | copy-start | bytes 3145732
  268.9 24.5 %all-to-all-start.2 = ((bf16[128,8,512]{2,1,0:T(8,128)(2,1)}), bf16[128,8,512]{2,1,0:T(8,128)(2,1)}, u32[]{:S(2)}, u32[]{:S(2)}) async-start(bf16[128,8,512]{2,1,0:T(8,128)(2,1)} %broadcast_in_dim.2), calls=%async_computation.2 | async-start | bytes 2097152 | tf_op jit(solution)/shard_map/all_to_all | solution.py:222
  274.6 1.6 copy-start.2
  276.2 1.6 copy-start.6
  277.8 1.2 copy-start.8

commit v5 on v4

v5 whole, which is shorter than its diff:
```python
import functools
import math

import jax
import jax.numpy as jnp
from jax import lax
from jax.experimental import pallas as pl
from jax.experimental.pallas import tpu as pltpu
from jax.sharding import PartitionSpec as P

D = 512
BLK = 128
BLK_DEV = 8
OWNERS = 128
NB = 64
K = 10
COLUMNS = BLK_DEV + NB
TAG = 16
PIECES = D // OWNERS
SENT = PIECES * NB + TAG
BATCH = 16
F32 = jnp.float32
BF16 = jnp.bfloat16


def dot(a, b):
    return lax.dot_general(a, b, (((1,), (0,)), ((), ())), preferred_element_type=F32)


def halves(values):
    upper = values.astype(BF16)
    return upper, (values - upper.astype(F32)).astype(BF16)


def whole(*shape):
    return pl.BlockSpec(shape, lambda *_: (0,) * len(shape))


def scatter_kernel(
    col_ref, counts_ref, preact_ref, cot_ref, feat_ref, tag_ref, own_ref, self_ref, send_ref, acc, stage, sems
):
    b = pl.program_id(0)

    @pl.when(b == 0)
    def _():
        acc[...] = jnp.zeros_like(acc)
        self_ref[...] = jnp.zeros_like(self_ref)

    counts = counts_ref[0].astype(F32)
    degree = 1.0 + jnp.sum(jnp.sum(counts, axis=0), axis=1, keepdims=True)
    root = jnp.broadcast_to(jnp.sqrt(degree), (BLK, BLK)).T[:1]
    grad = jnp.where(preact_ref[...] > 0, cot_ref[...], 0.0).T
    both = jnp.concatenate(halves(grad), axis=1)
    feat = feat_ref[...]
    self_ref[...] += dot(both, jnp.concatenate([feat, feat], axis=0))
    both = jnp.concatenate(halves(grad / root), axis=1)
    tiles = counts.astype(BF16)

    def column(c):
        return pl.ds(pl.multiple_of(c * D, D), D)

    for t in range(0, K, 2):
        pair = jnp.concatenate([tiles[t], tiles[t + 1]], axis=1)
        part = dot(both, jnp.concatenate([pair, pair], axis=0))
        acc[column(col_ref[b, t])] += part[:, :BLK]
        acc[column(col_ref[b, t + 1])] += part[:, BLK:]

    @pl.when(b == BLK_DEV - 1)
    def _():
        def put(g):
            rows = pl.ds(g * BATCH, BATCH)
            return pltpu.make_async_copy(stage.at[rows], send_ref.at[rows], sems.at[g])

        @pl.loop(0, OWNERS // BATCH)
        def _(g):
            @pl.loop(0, BATCH)
            def _(i):
                j = g * BATCH + i
                for r in range(PIECES):
                    start = BLK_DEV * D + r * OWNERS + j
                    stage[j, r * NB : (r + 1) * NB] = acc[pl.ds(start, NB, stride=D)].astype(BF16)
                stage[j, PIECES * NB :] = tag_ref[...]

            put(g).start()

        own_ref[...] = acc[: BLK_DEV * D].reshape(BLK_DEV, D, BLK)
        self_ref[...] = self_ref[...].T

        @pl.loop(0, OWNERS // BATCH)
        def _(g):
            put(g).wait()


def partials(tile_col, counts, preact, cotangent, features, tag):
    rows = pl.BlockSpec((BLK, D), lambda b, *_: (b, 0))
    return pl.pallas_call(
        scatter_kernel,
        grid_spec=pltpu.PrefetchScalarGridSpec(
            num_scalar_prefetch=1,
            grid=(BLK_DEV,),
            in_specs=[
                pl.BlockSpec((1, K, BLK, BLK), lambda b, *_: (b, 0, 0, 0)),
                rows,
                rows,
                rows,
                whole(TAG, BLK),
            ],
            out_specs=[whole(BLK_DEV, D, BLK), whole(D, D), pl.BlockSpec(memory_space=pl.ANY)],
            scratch_shapes=[
                pltpu.VMEM((COLUMNS * D, BLK), F32),
                pltpu.VMEM((OWNERS, SENT, BLK), BF16),
                pltpu.SemaphoreType.DMA((OWNERS // BATCH,)),
            ],
        ),
        out_shape=[
            jax.ShapeDtypeStruct((BLK_DEV, D, BLK), F32),
            jax.ShapeDtypeStruct((D, D), F32),
            jax.ShapeDtypeStruct((OWNERS, SENT, BLK), BF16),
        ],
        compiler_params=pltpu.CompilerParams(vmem_limit_bytes=58 << 20),
        cost_estimate=pl.CostEstimate(
            flops=4 * BLK_DEV * K * BLK * BLK * D, bytes_accessed=22 << 20, transcendentals=0
        ),
    )(tile_col, counts, preact, cotangent, features, tag)


GROUP = 16
STEPS = OWNERS // GROUP
BINS = OWNERS * BLK_DEV
MERGED = 256


def merge_kernel(ids_ref, recv_ref, out_ref, acc):
    step = pl.program_id(0)

    @pl.when(step == 0)
    def _():
        acc[...] = jnp.zeros_like(acc)

    pieces = [recv_ref[:, r * NB : (r + 1) * NB].reshape(GROUP * NB, BLK) for r in range(PIECES)]
    values = jnp.concatenate(pieces, axis=1)
    rows = lax.broadcasted_iota(jnp.int32, (MERGED, BLK), 0)
    for m in range(0, BINS, MERGED):
        hot = [
            jnp.where(rows == ids_ref[p : p + 1] - m, 1.0, 0.0).astype(BF16) for p in range(GROUP // 2)
        ]
        acc[m : m + MERGED] += dot(jnp.concatenate(hot, axis=1), values)

    @pl.when(step == STEPS - 1)
    def _():
        out_ref[...] = acc[...].astype(BF16)


def merged(ids, received):
    return pl.pallas_call(
        merge_kernel,
        grid=(STEPS,),
        in_specs=[
            pl.BlockSpec((GROUP // 2, BLK), lambda s: (s, 0)),
            pl.BlockSpec((GROUP, SENT, BLK), lambda s: (s, 0, 0)),
        ],
        out_specs=whole(BINS, PIECES * BLK),
        out_shape=jax.ShapeDtypeStruct((BINS, PIECES * BLK), BF16),
        scratch_shapes=[pltpu.VMEM((BINS, PIECES * BLK), F32)],
        compiler_params=pltpu.CompilerParams(vmem_limit_bytes=24 << 20),
        cost_estimate=pl.CostEstimate(
            flops=2 * BINS * OWNERS * NB * PIECES * BLK, bytes_accessed=10 << 20, transcendentals=0
        ),
    )(ids, received)


def total_kernel(recv_ref, own_ref, feat_ref, self_ref, total_ref, joined_ref, flat):
    arrived = recv_ref[...].astype(F32).reshape(BINS, PIECES * BLK)
    for r in range(PIECES):
        flat[r * BINS : (r + 1) * BINS] = arrived[:, r * BLK : (r + 1) * BLK]
    for g in range(BLK_DEV):
        for r in range(PIECES):
            rows = slice(r * OWNERS, (r + 1) * OWNERS)
            part = flat[pl.ds(r * BINS + g, OWNERS, stride=BLK_DEV)]
            total_ref[g, rows] = own_ref[g, rows] + part
    neigh = jnp.zeros((D, D), F32)
    for g in range(0, BLK_DEV, 2):
        upper, lower = halves(jnp.concatenate([total_ref[g], total_ref[g + 1]], axis=1))
        feat = feat_ref[g * BLK : (g + 2) * BLK, :]
        neigh += dot(upper, feat) + dot(lower, feat)
    joined_ref[:D] = self_ref[...].astype(BF16)
    joined_ref[D:] = neigh.T.astype(BF16)


def totals(received, own, features, self_part):
    return pl.pallas_call(
        total_kernel,
        in_specs=[pl.BlockSpec(memory_space=pltpu.VMEM)] * 4,
        out_specs=[pl.BlockSpec(memory_space=pltpu.VMEM)] * 2,
        out_shape=[
            jax.ShapeDtypeStruct((BLK_DEV, D, BLK), F32),
            jax.ShapeDtypeStruct((2 * D, D), BF16),
        ],
        scratch_shapes=[pltpu.VMEM((PIECES * BINS, BLK), F32)],
        compiler_params=pltpu.CompilerParams(vmem_limit_bytes=24 << 20),
        cost_estimate=pl.CostEstimate(
            flops=4 * BLK_DEV * BLK * D * D, bytes_accessed=8 << 20, transcendentals=0
        ),
    )(received, own, features, self_part)


def feature_kernel(total_ref, preact_ref, cot_ref, self_ref, neigh_ref, grad_ref):
    grad = jnp.where(preact_ref[...] > 0, cot_ref[...], 0.0)
    upper, lower = halves(grad)
    w_upper, w_lower = halves(self_ref[...].T)
    result = dot(upper, w_upper) + dot(lower, w_upper) + dot(upper, w_lower)
    upper, lower = halves(jnp.concatenate([total_ref[0], total_ref[1]], axis=1).T)
    w_upper, w_lower = halves(neigh_ref[...].T)
    grad_ref[...] = result + (dot(upper, w_upper) + dot(lower, w_upper) + dot(upper, w_lower))


def feature_gradient(total, preact, cotangent, w_self, w_neigh):
    rows = pl.BlockSpec((2 * BLK, D), lambda g: (g, 0))
    return pl.pallas_call(
        feature_kernel,
        grid=(BLK_DEV // 2,),
        in_specs=[pl.BlockSpec((2, D, BLK), lambda g: (g, 0, 0)), rows, rows, whole(D, D), whole(D, D)],
        out_specs=rows,
        out_shape=jax.ShapeDtypeStruct((BLK_DEV * BLK, D), F32),
        compiler_params=pltpu.CompilerParams(vmem_limit_bytes=16 << 20),
        cost_estimate=pl.CostEstimate(
            flops=12 * BLK_DEV * BLK * D * D, bytes_accessed=10 << 20, transcendentals=0
        ),
    )(total, preact, cotangent, w_self, w_neigh)


def list_rows(owner, slot):
    lists = jnp.concatenate([owner, slot], axis=0)
    return jnp.pad(jnp.tile(lists, (1, BLK // NB)), ((0, TAG - 2), (0, 0))).astype(BF16)


def block_numbers(received):
    lists = received[:, PIECES * NB : PIECES * NB + 2].astype(jnp.int32)
    numbers = (lists[:, 0] * BLK_DEV + lists[:, 1]).reshape(OWNERS // 2, 2, BLK)
    lanes = lax.broadcasted_iota(jnp.int32, (OWNERS // 2, BLK), 1)
    return jnp.where(lanes < NB, numbers[:, 0], numbers[:, 1])


def shards(features, preact, cotangent, w_self, w_neigh, tile_counts, tile_col, owner, slot):
    own, self_part, outgoing = partials(
        tile_col, tile_counts, preact, cotangent, features, list_rows(owner, slot)
    )
    received = lax.all_to_all(outgoing, "nodes", 0, 0, tiled=True)
    sums = merged(block_numbers(received), received).reshape(OWNERS, BLK_DEV, PIECES * BLK)
    sums = lax.all_to_all(sums, "nodes", 0, 0, tiled=True)
    total, joined = totals(sums, own, features, self_part)

    rows = 2 * D // OWNERS
    shares = lax.all_to_all(joined.reshape(OWNERS, rows, D), "nodes", 0, 0, tiled=True)
    share = jnp.sum(shares.astype(F32), axis=0).astype(BF16)
    share, total = lax.optimization_barrier((share, total))
    spread = jnp.broadcast_to(share[None], (OWNERS, rows, D))
    both = lax.all_to_all(spread, "nodes", 0, 0, tiled=True).reshape(2 * D, D)
    grad_features = feature_gradient(total, preact, cotangent, w_self, w_neigh)
    scale = 1.0 / math.sqrt(OWNERS * BLK_DEV * BLK)
    return grad_features, both[:D].astype(F32) * scale, both[D:].astype(F32) * scale


def solution(mesh):
    rows = P("nodes", None)
    return jax.shard_map(
        shards,
        mesh=mesh,
        in_specs=(rows, rows, rows, P(), P(), P("nodes", None, None, None), rows, rows, rows),
        out_specs=(rows, P(), P()),
        check_vma=False,
    )
```

time: 297 us -> 257 us (0.87)
  blocking collectives: 239 us -> 51.2 us
  waiting for transfers between devices: 8.6 us -> 121 us
  Pallas kernels: 28.5 us -> 51.9 us
  starting transfers between devices: 5.64 us -> 17.5 us
    all_to_all x1, blocking collectives: 212 us -> 27.4 us  [shards(): sums = lax.all_to_all(sums, 'nodes', 0, 0, tiled=True)]
    all_to_all x0 -> x1, waiting for transfers between devices: none -> 113 us  [shards(): received = lax.all_to_all(outgoing, 'nodes', 0, 0, tiled=True)]
    pallas_call x1, Pallas kernels: 17.5 us -> 32.8 us  [partials(): pl.pallas_call(scatter_kernel, grid_spec=pltpu.PrefetchScalarGridSpec(num...]
    all_to_all x0 -> x1, starting transfers between devices: none -> 11.9 us  [shards(): received = lax.all_to_all(outgoing, 'nodes', 0, 0, tiled=True)]
    pallas_call x1 -> x2, Pallas kernels: 5.18 us -> 13.3 us  [the longest x1 11.8 us: merged(): pl.pallas_call(merge_kernel, grid=(STEPS,), in_specs=[pl.BlockSpec((GROUP...]
    all_to_all x1, blocking collectives: 27.2 us -> 23.8 us  [shards(): lax.all_to_all(joined.reshape(OWNERS, rows, D), 'nodes', 0, 0, tiled=True)]
  transfers between devices with their start and end apart: 1 -> 2, of which waited for: 1 -> 2; matrix products, arithmetic and copies ran while one was open for 0% -> 0% of each run, Pallas kernels for 2% -> 2%
where the time goes in v5:
time: 257 us; the launch traced here: 256 us
  waiting for transfers between devices  121 us (47%)
  Pallas kernels  51.9 us (20%)
  blocking collectives  51.2 us (20%)
  starting transfers between devices  17.5 us (7%)
  local copies, waits for them, and re-layouts  7.53 us (3%)
  other arithmetic  6.16 us (2%)
    all_to_all x1, waiting for transfers between devices, shards(): received = lax.all_to_all(outgoing, 'nodes', 0, 0, tiled=True)  113 us
    pallas_call x1, Pallas kernels, partials(): pl.pallas_call(scatter_kernel, grid_spec=pltpu.PrefetchScalarGridSpec(num...  32.8 us
    all_to_all x1, blocking collectives, shards(): sums = lax.all_to_all(sums, 'nodes', 0, 0, tiled=True)  27.4 us
    all_to_all x1, blocking collectives, shards(): lax.all_to_all(joined.reshape(OWNERS, rows, D), 'nodes', 0, 0, tiled=True)  23.8 us
    all_to_all x1, starting transfers between devices, shards(): received = lax.all_to_all(outgoing, 'nodes', 0, 0, tiled=True)  11.9 us
    pallas_call x1, Pallas kernels, merged(): pl.pallas_call(merge_kernel, grid=(STEPS,), in_specs=[pl.BlockSpec((GROUP...  11.8 us
    all_to_all x1, waiting for transfers between devices, shards(): both = lax.all_to_all(spread, 'nodes', 0, 0, tiled=True).reshape(2 * D, D)  8.61 us
    pallas_call x1, Pallas kernels, feature_gradient(): pl.pallas_call(feature_kernel, grid=(BLK_DEV // 2,), in_specs=[pl.BlockSp...  5.82 us
  transfers between devices with their start and end apart: 2, of which 2 were waited for; matrix products, arithmetic and copies ran while one was open for 0% of the time, Pallas kernels for 2%

profile of v5, /device:TPU:1, one launch (start us, length us, event | category | flops | bytes accessed | tf_op | source)
XLA Modules:
  0.0 256.4 jit_solution(10778630055245285043)
XLA Ops:
  0.6 0.7 add_convert_fusion
  1.3 0.1 tile.11
  1.4 0.6 pad.5.tag_ref
  2.0 32.8 %shard_map.112 = (f32[8,512,128]{2,1,0:T(8,128)}, f32[512,512]{1,0:T(8,128)}, bf16[128,272,128]{2,1,0:T(8,128)(2,1)}) custom-call(s32[8,10]{1,0:T(8,128)} %col_ref.1, s32[8,10,128,128]{3,2,1,0:T(8,128)} %counts_ref.1, f32[1024,512]{1,0:T(8,128)} %preact_ref.3, f32[1024,512]{1,0:T(8,128)} %cot_ref.3, bf16[1024,512]{1,0:T(8,128)(2,1)} %feat_ref.3, ...), custom_call_target="tpu_custom_call" | custom-call | flops 2684354560 | bytes 23068672 | tf_op jit(solution)/shard_map/pallas_call | solution.py:96
  34.8 11.9 %all-to-all-start = ((bf16[128,272,128]{2,1,0:T(8,128)(2,1)}), bf16[128,272,128]{2,1,0:T(8,128)(2,1)}, u32[]{:S(2)}, u32[]{:S(2)}) async-start(bf16[128,272,128]{2,1,0:T(8,128)(2,1)} %get-tuple-element.10), calls=%async_computation | async-start | bytes 17825792 | tf_op jit(solution)/shard_map/all_to_all | solution.py:248
  46.7 112.6 %all-to-all-done.recv_ref = bf16[128,272,128]{2,1,0:T(8,128)(2,1)} async-done(((bf16[128,272,128]{2,1,0:T(8,128)(2,1)}), bf16[128,272,128]{2,1,0:T(8,128)(2,1)}, u32[]{:S(2)}, u32[]{:S(2)}) %all-to-all-start) | async-done | bytes 8912928 | tf_op jit(solution)/shard_map/all_to_all | solution.py:248
  159.3 1.0 slice_convert_fusion
  160.3 0.1 slice_add_fusion
  160.4 0.1 fusion
  160.5 0.0 copy-start.1
  160.5 11.8 %shard_map.113 = bf16[1024,512]{1,0:T(8,128)(2,1)S(1)} custom-call(s32[64,128]{1,0:T(8,128)S(1)} %broadcast_select_fusion.ids_ref, bf16[128,272,128]{2,1,0:T(8,128)(2,1)} %all-to-all-done.recv_ref), custom_call_target="tpu_custom_call" | custom-call | flops 8589934592 | bytes 10485760 | tf_op jit(solution)/shard_map/pallas_call | solution.py:155
  172.3 0.0 copy-start
  172.3 0.0 copy-start.4
  172.4 27.4 %all_to_all.20.recv_ref = bf16[128,8,512]{2,1,0:T(8,128)(2,1)S(1)} all-to-all(bf16[128,8,512]{2,1,0:T(8,128)(2,1)S(1)} %bitcast.14), channel_id=1, replica_groups=mesh['nodes'=128] {'nodes'}, dimensions={0} | all-to-all | bytes 2097152 | tf_op jit(solution)/shard_map/all_to_all | solution.py:250
  199.8 0.0 copy-done.1
  199.8 0.0 copy-done
  199.8 0.0 copy-done.4
  199.8 1.5 shard_map.114
  201.3 0.0 copy-start.5
  201.3 1.3 copy-done.5
  202.6 23.8 %all_to_all.21 = bf16[128,8,512]{2,1,0:T(8,128)(2,1)} all-to-all(bf16[128,8,512]{2,1,0:T(8,128)(2,1)S(1)} %bitcast.13), channel_id=1, replica_groups=mesh['nodes'=128] {'nodes'}, dimensions={0} | all-to-all | bytes 2097152 | tf_op jit(solution)/shard_map/all_to_all | solution.py:254
  226.4 0.0 copy-start.2
  226.4 0.0 copy-start.7
  226.4 1.6 reduce_sum.12
  228.0 1.0 broadcast_in_dim.2
  229.0 5.6 %all-to-all-start.3 = ((bf16[128,8,512]{2,1,0:T(8,128)(2,1)}), bf16[128,8,512]{2,1,0:T(8,128)(2,1)}, u32[]{:S(2)}, u32[]{:S(2)}) async-start(bf16[128,8,512]{2,1,0:T(8,128)(2,1)} %broadcast_in_dim.2), calls=%async_computation.3 | async-start | bytes 2097152 | tf_op jit(solution)/shard_map/all_to_all | solution.py:258
  234.7 0.0 copy-done.2
  234.7 0.0 copy-done.7
  234.7 0.0 copy-start.3
  234.7 1.6 copy-done.3
  236.3 0.0 copy-start.6
  236.3 1.6 copy-done.6
  237.9 0.0 copy-start.8
  237.9 1.2 copy-done.8
  239.1 5.8 %shard_map.115 = f32[1024,512]{1,0:T(8,128)} custom-call(f32[8,512,128]{2,1,0:T(8,128)S(1)} %copy-done.6, f32[1024,512]{1,0:T(8,128)S(1)} %copy-done.2, f32[1024,512]{1,0:T(8,128)S(1)} %copy-done.3, f32[512,512]{1,0:T(8,128)S(1)} %copy-done.7, f32[512,512]{1,0:T(8,128)S(1)} %copy-done.8), custom_call_target="tpu_custom_call" | custom-call | flops 3221225472 | bytes 10485760 | tf_op jit(solution)/shard_map/pallas_call | solution.py:219
  244.9 8.6 %all-to-all-done.3 = bf16[128,8,512]{2,1,0:T(8,128)(2,1)} async-done(((bf16[128,8,512]{2,1,0:T(8,128)(2,1)}), bf16[128,8,512]{2,1,0:T(8,128)(2,1)}, u32[]{:S(2)}, u32[]{:S(2)}) %all-to-all-start.3) | async-done | bytes 1048608 | tf_op jit(solution)/shard_map/all_to_all | solution.py:258
  253.5 2.8 %multiply_bitcast_fusion = (f32[512,512]{1,0:T(8,128)}, f32[512,512]{1,0:T(8,128)}) fusion(bf16[128,8,512]{2,1,0:T(8,128)(2,1)} %all-to-all-done.3), kind=kLoop, calls=%fused_computation | loop fusion | flops 1048576 | bytes 3145728 | tf_op jit(solution)/shard_map/mul | solution.py:261
  (3 shorter events, 0.0 us)
Async XLA Ops:
  34.8 124.5 %all-to-all-start = ((bf16[128,272,128]{2,1,0:T(8,128)(2,1)}), bf16[128,272,128]{2,1,0:T(8,128)(2,1)}, u32[]{:S(2)}, u32[]{:S(2)}) async-start(bf16[128,272,128]{2,1,0:T(8,128)(2,1)} %get-tuple-element.10), calls=%async_computation | async-start | bytes 17825792 | tf_op jit(solution)/shard_map/all_to_all | solution.py:248
  160.5 39.3 %copy-start.1 = (f32[8,512,128]{2,1,0:T(8,128)S(1)}, f32[8,512,128]{2,1,0:T(8,128)}, u32[]{:S(2)}) copy-start(f32[8,512,128]{2,1,0:T(8,128)} %get-tuple-element.11.own_ref) | copy-start | bytes 6291460
  172.3 27.4 %copy-start = (bf16[1024,512]{1,0:T(8,128)(2,1)S(1)}, bf16[1024,512]{1,0:T(8,128)(2,1)}, u32[]{:S(2)}) copy-start(bf16[1024,512]{1,0:T(8,128)(2,1)} %feat_ref.3) | copy-start | bytes 3145732
  172.3 27.4 %copy-start.4 = (f32[512,512]{1,0:T(8,128)S(1)}, f32[512,512]{1,0:T(8,128)}, u32[]{:S(2)}) copy-start(f32[512,512]{1,0:T(8,128)} %get-tuple-element.12.self_ref) | copy-start | bytes 3145732
  201.3 1.3 copy-start.5
  226.4 8.3 %copy-start.2 = (f32[1024,512]{1,0:T(8,128)S(1)}, f32[1024,512]{1,0:T(8,128)}, u32[]{:S(2)}) copy-start(f32[1024,512]{1,0:T(8,128)} %preact_ref.3) | copy-start | bytes 6291460
  226.4 8.3 %copy-start.7 = (f32[512,512]{1,0:T(8,128)S(1)}, f32[512,512]{1,0:T(8,128)}, u32[]{:S(2)}) copy-start(f32[512,512]{1,0:T(8,128)} %self_ref.1) | copy-start | bytes 3145732
  229.0 24.5 %all-to-all-start.3 = ((bf16[128,8,512]{2,1,0:T(8,128)(2,1)}), bf16[128,8,512]{2,1,0:T(8,128)(2,1)}, u32[]{:S(2)}, u32[]{:S(2)}) async-start(bf16[128,8,512]{2,1,0:T(8,128)(2,1)} %broadcast_in_dim.2), calls=%async_computation.3 | async-start | bytes 2097152 | tf_op jit(solution)/shard_map/all_to_all | solution.py:258
  234.7 1.6 copy-start.3
  236.3 1.6 copy-start.6
  237.9 1.2 copy-start.8

commit v6 on v5

--- a/solution.py
+++ b/solution.py
@@ -19,6 +19,7 @@
 PIECES = D // OWNERS
 SENT = PIECES * NB + TAG
 BATCH = 16
+PITCH = D + 8
 F32 = jnp.float32
 BF16 = jnp.bfloat16
 
@@ -57,7 +58,7 @@
     tiles = counts.astype(BF16)
 
     def column(c):
-        return pl.ds(pl.multiple_of(c * D, D), D)
+        return pl.ds(pl.multiple_of(c * PITCH, 8), D)
 
     for t in range(0, K, 2):
         pair = jnp.concatenate([tiles[t], tiles[t + 1]], axis=1)
@@ -77,13 +78,14 @@
             def _(i):
                 j = g * BATCH + i
                 for r in range(PIECES):
-                    start = BLK_DEV * D + r * OWNERS + j
-                    stage[j, r * NB : (r + 1) * NB] = acc[pl.ds(start, NB, stride=D)].astype(BF16)
+                    start = BLK_DEV * PITCH + r * OWNERS + j
+                    stage[j, r * NB : (r + 1) * NB] = acc[pl.ds(start, NB, stride=PITCH)].astype(BF16)
                 stage[j, PIECES * NB :] = tag_ref[...]
 
             put(g).start()
 
-        own_ref[...] = acc[: BLK_DEV * D].reshape(BLK_DEV, D, BLK)
+        for c in range(BLK_DEV):
+            own_ref[c] = acc[c * PITCH : c * PITCH + D]
         self_ref[...] = self_ref[...].T
 
         @pl.loop(0, OWNERS // BATCH)
@@ -107,7 +109,7 @@
             ],
             out_specs=[whole(BLK_DEV, D, BLK), whole(D, D), pl.BlockSpec(memory_space=pl.ANY)],
             scratch_shapes=[
-                pltpu.VMEM((COLUMNS * D, BLK), F32),
+                pltpu.VMEM((COLUMNS * PITCH, BLK), F32),
                 pltpu.VMEM((OWNERS, SENT, BLK), BF16),
                 pltpu.SemaphoreType.DMA((OWNERS // BATCH,)),
             ],
@@ -130,7 +132,7 @@
 MERGED = 256
 
 
-def merge_kernel(ids_ref, recv_ref, out_ref, acc):
+def merge_kernel(recv_ref, out_ref, acc):
     step = pl.program_id(0)
 
     @pl.when(step == 0)
@@ -139,11 +141,13 @@
 
     pieces = [recv_ref[:, r * NB : (r + 1) * NB].reshape(GROUP * NB, BLK) for r in range(PIECES)]
     values = jnp.concatenate(pieces, axis=1)
+    lists = [recv_ref[i, PIECES * NB :].astype(F32) for i in range(GROUP)]
+    numbers = [rows[:1] * BLK_DEV + rows[1:2] for rows in lists]
+    first = lax.broadcasted_iota(jnp.int32, (1, BLK), 1) < NB
+    pairs = [jnp.where(first, numbers[i], numbers[i + 1]).astype(jnp.int32) for i in range(0, GROUP, 2)]
     rows = lax.broadcasted_iota(jnp.int32, (MERGED, BLK), 0)
     for m in range(0, BINS, MERGED):
-        hot = [
-            jnp.where(rows == ids_ref[p : p + 1] - m, 1.0, 0.0).astype(BF16) for p in range(GROUP // 2)
-        ]
+        hot = [jnp.where(rows == pair - m, 1.0, 0.0).astype(BF16) for pair in pairs]
         acc[m : m + MERGED] += dot(jnp.concatenate(hot, axis=1), values)
 
     @pl.when(step == STEPS - 1)
@@ -151,14 +155,11 @@
         out_ref[...] = acc[...].astype(BF16)
 
 
-def merged(ids, received):
+def merged(received):
     return pl.pallas_call(
         merge_kernel,
         grid=(STEPS,),
-        in_specs=[
-            pl.BlockSpec((GROUP // 2, BLK), lambda s: (s, 0)),
-            pl.BlockSpec((GROUP, SENT, BLK), lambda s: (s, 0, 0)),
-        ],
+        in_specs=[pl.BlockSpec((GROUP, SENT, BLK), lambda s: (s, 0, 0))],
         out_specs=whole(BINS, PIECES * BLK),
         out_shape=jax.ShapeDtypeStruct((BINS, PIECES * BLK), BF16),
         scratch_shapes=[pltpu.VMEM((BINS, PIECES * BLK), F32)],
@@ -166,79 +167,105 @@
         cost_estimate=pl.CostEstimate(
             flops=2 * BINS * OWNERS * NB * PIECES * BLK, bytes_accessed=10 << 20, transcendentals=0
         ),
-    )(ids, received)
-
-
-def total_kernel(recv_ref, own_ref, feat_ref, self_ref, total_ref, joined_ref, flat):
+    )(received)
+
+
+def add_own(recv_ref, own_ref, flat, total):
     arrived = recv_ref[...].astype(F32).reshape(BINS, PIECES * BLK)
     for r in range(PIECES):
         flat[r * BINS : (r + 1) * BINS] = arrived[:, r * BLK : (r + 1) * BLK]
     for g in range(BLK_DEV):
         for r in range(PIECES):
             rows = slice(r * OWNERS, (r + 1) * OWNERS)
-            part = flat[pl.ds(r * BINS + g, OWNERS, stride=BLK_DEV)]
-            total_ref[g, rows] = own_ref[g, rows] + part
+            total[g, rows] = own_ref[g, rows] + flat[pl.ds(r * BINS + g, OWNERS, stride=BLK_DEV)]
+
+
+def neigh_kernel(recv_ref, own_ref, feat_ref, self_ref, joined_ref, flat, total):
+    add_own(recv_ref, own_ref, flat, total)
     neigh = jnp.zeros((D, D), F32)
     for g in range(0, BLK_DEV, 2):
-        upper, lower = halves(jnp.concatenate([total_ref[g], total_ref[g + 1]], axis=1))
+        upper, lower = halves(jnp.concatenate([total[g], total[g + 1]], axis=1))
         feat = feat_ref[g * BLK : (g + 2) * BLK, :]
         neigh += dot(upper, feat) + dot(lower, feat)
     joined_ref[:D] = self_ref[...].astype(BF16)
     joined_ref[D:] = neigh.T.astype(BF16)
 
 
-def totals(received, own, features, self_part):
-    return pl.pallas_call(
-        total_kernel,
-        in_specs=[pl.BlockSpec(memory_space=pltpu.VMEM)] * 4,
-        out_specs=[pl.BlockSpec(memory_space=pltpu.VMEM)] * 2,
-        out_shape=[
-            jax.ShapeDtypeStruct((BLK_DEV, D, BLK), F32),
-            jax.ShapeDtypeStruct((2 * D, D), BF16),
-        ],
-        scratch_shapes=[pltpu.VMEM((PIECES * BINS, BLK), F32)],
+VMEM_SPEC = pl.BlockSpec(memory_space=pltpu.VMEM)
+TOTAL_SCRATCH = [pltpu.VMEM((PIECES * BINS, BLK), F32), pltpu.VMEM((BLK_DEV, D, BLK), F32)]
+
+
+def weight_gradients(received, own, features, self_part):
+    return pl.pallas_call(
+        neigh_kernel,
+        in_specs=[VMEM_SPEC] * 4,
+        out_specs=VMEM_SPEC,
+        out_shape=jax.ShapeDtypeStruct((2 * D, D), BF16),
+        scratch_shapes=TOTAL_SCRATCH,
         compiler_params=pltpu.CompilerParams(vmem_limit_bytes=24 << 20),
         cost_estimate=pl.CostEstimate(
-            flops=4 * BLK_DEV * BLK * D * D, bytes_accessed=8 << 20, transcendentals=0
+            flops=4 * BLK_DEV * BLK * D * D, bytes_accessed=6 << 20, transcendentals=0
         ),
     )(received, own, features, self_part)
 
 
-def feature_kernel(total_ref, preact_ref, cot_ref, self_ref, neigh_ref, grad_ref):
+def share_kernel(shares_ref, spread_ref):
+    share = jnp.sum(shares_ref[...].astype(F32), axis=0, keepdims=True).astype(BF16)
+    spread_ref[...] = jnp.broadcast_to(share, spread_ref.shape)
+
+
+def added_up(shares):
+    return pl.pallas_call(
+        share_kernel,
+        in_specs=[VMEM_SPEC],
+        out_specs=VMEM_SPEC,
+        out_shape=jax.ShapeDtypeStruct(shares.shape, BF16),
+        compiler_params=pltpu.CompilerParams(vmem_limit_bytes=16 << 20),
+    )(shares)
+
+
+def feature_kernel(recv_ref, own_ref, preact_ref, cot_ref, self_ref, neigh_ref, grad_ref, flat, total):
+    g = pl.program_id(0)
+
+    @pl.when(g == 0)
+    def _():
+        add_own(recv_ref, own_ref, flat, total)
+
     grad = jnp.where(preact_ref[...] > 0, cot_ref[...], 0.0)
     upper, lower = halves(grad)
     w_upper, w_lower = halves(self_ref[...].T)
     result = dot(upper, w_upper) + dot(lower, w_upper) + dot(upper, w_lower)
-    upper, lower = halves(jnp.concatenate([total_ref[0], total_ref[1]], axis=1).T)
+    upper, lower = halves(jnp.concatenate([total[2 * g], total[2 * g + 1]], axis=1).T)
     w_upper, w_lower = halves(neigh_ref[...].T)
     grad_ref[...] = result + (dot(upper, w_upper) + dot(lower, w_upper) + dot(upper, w_lower))
 
 
-def feature_gradient(total, preact, cotangent, w_self, w_neigh):
+def feature_gradient(received, own, preact, cotangent, w_self, w_neigh):
     rows = pl.BlockSpec((2 * BLK, D), lambda g: (g, 0))
     return pl.pallas_call(
         feature_kernel,
         grid=(BLK_DEV // 2,),
-        in_specs=[pl.BlockSpec((2, D, BLK), lambda g: (g, 0, 0)), rows, rows, whole(D, D), whole(D, D)],
+        in_specs=[
+            whole(OWNERS, BLK_DEV, PIECES * BLK),
+            whole(BLK_DEV, D, BLK),
+            rows,
+            rows,
+            whole(D, D),
+            whole(D, D),
+        ],
         out_specs=rows,
         out_shape=jax.ShapeDtypeStruct((BLK_DEV * BLK, D), F32),
-        compiler_params=pltpu.CompilerParams(vmem_limit_bytes=16 << 20),
+        scratch_shapes=TOTAL_SCRATCH,
+        compiler_params=pltpu.CompilerParams(vmem_limit_bytes=32 << 20),
         cost_estimate=pl.CostEstimate(
             flops=12 * BLK_DEV * BLK * D * D, bytes_accessed=10 << 20, transcendentals=0
         ),
-    )(total, preact, cotangent, w_self, w_neigh)
+    )(received, own, preact, cotangent, w_self, w_neigh)
 
 
 def list_rows(owner, slot):
     lists = jnp.concatenate([owner, slot], axis=0)
     return jnp.pad(jnp.tile(lists, (1, BLK // NB)), ((0, TAG - 2), (0, 0))).astype(BF16)
-
-
-def block_numbers(received):
-    lists = received[:, PIECES * NB : PIECES * NB + 2].astype(jnp.int32)
-    numbers = (lists[:, 0] * BLK_DEV + lists[:, 1]).reshape(OWNERS // 2, 2, BLK)
-    lanes = lax.broadcasted_iota(jnp.int32, (OWNERS // 2, BLK), 1)
-    return jnp.where(lanes < NB, numbers[:, 0], numbers[:, 1])
 
 
 def shards(features, preact, cotangent, w_self, w_neigh, tile_counts, tile_col, owner, slot):
@@ -246,17 +273,15 @@
         tile_col, tile_counts, preact, cotangent, features, list_rows(owner, slot)
     )
     received = lax.all_to_all(outgoing, "nodes", 0, 0, tiled=True)
-    sums = merged(block_numbers(received), received).reshape(OWNERS, BLK_DEV, PIECES * BLK)
+    sums = merged(received).reshape(OWNERS, BLK_DEV, PIECES * BLK)
     sums = lax.all_to_all(sums, "nodes", 0, 0, tiled=True)
-    total, joined = totals(sums, own, features, self_part)
+    joined = weight_gradients(sums, own, features, self_part)
 
     rows = 2 * D // OWNERS
     shares = lax.all_to_all(joined.reshape(OWNERS, rows, D), "nodes", 0, 0, tiled=True)
-    share = jnp.sum(shares.astype(F32), axis=0).astype(BF16)
-    share, total = lax.optimization_barrier((share, total))
-    spread = jnp.broadcast_to(share[None], (OWNERS, rows, D))
+    spread, sums = lax.optimization_barrier((added_up(shares), sums))
     both = lax.all_to_all(spread, "nodes", 0, 0, tiled=True).reshape(2 * D, D)
-    grad_features = feature_gradient(total, preact, cotangent, w_self, w_neigh)
+    grad_features = feature_gradient(sums, own, preact, cotangent, w_self, w_neigh)
     scale = 1.0 / math.sqrt(OWNERS * BLK_DEV * BLK)
     return grad_features, both[:D].astype(F32) * scale, both[D:].astype(F32) * scale
 

time: 257 us -> 229 us (0.89)
  blocking collectives: 51.2 us -> 166 us
  waiting for transfers between devices: 121 us -> 6.68 us
  Pallas kernels: 51.9 us -> 39.3 us
  starting transfers between devices: 17.5 us -> 5.64 us
  other arithmetic: 6.16 us -> 3.49 us
    all_to_all x0 -> x1, blocking collectives: none -> 117 us  [shards(): received = lax.all_to_all(outgoing, 'nodes', 0, 0, tiled=True)]
    all_to_all x1 -> x0, waiting for transfers between devices: 113 us -> none  [shards(): received = lax.all_to_all(outgoing, 'nodes', 0, 0, tiled=True)]
    pallas_call x1, Pallas kernels: 32.8 us -> 19.8 us  [partials(): pl.pallas_call(scatter_kernel, grid_spec=pltpu.PrefetchScalarGridSpec(num...]
    all_to_all x1 -> x0, starting transfers between devices: 11.9 us -> none  [shards(): received = lax.all_to_all(outgoing, 'nodes', 0, 0, tiled=True)]
    pallas_call x2 -> x3, Pallas kernels: 7.31 us -> 9.19 us  [the longest x1 6.55 us: feature_gradient(): pl.pallas_call(feature_kernel, grid=(BLK_DEV // 2,), in_specs=[whole(OWNE...]
    unnamed x18 -> x14, local copies, waits for them, and re-layouts: 5.74 us -> 5.64 us
  transfers between devices with their start and end apart: 2 -> 1, of which waited for: 2 -> 1; matrix products, arithmetic and copies ran while one was open for 0% -> 0% of each run, Pallas kernels for 2% -> 3%
where the time goes in v6:
time: 229 us; the launch traced here: 228 us
  blocking collectives  166 us (72%)
  Pallas kernels  39.3 us (17%)
  waiting for transfers between devices  6.68 us (3%)
  local copies, waits for them, and re-layouts  6.33 us (3%)
  starting transfers between devices  5.64 us (2%)
  other arithmetic  3.49 us (2%)
    all_to_all x1, blocking collectives, shards(): received = lax.all_to_all(outgoing, 'nodes', 0, 0, tiled=True)  117 us
    all_to_all x1, blocking collectives, shards(): sums = lax.all_to_all(sums, 'nodes', 0, 0, tiled=True)  25.7 us
    all_to_all x1, blocking collectives, shards(): lax.all_to_all(joined.reshape(OWNERS, rows, D), 'nodes', 0, 0, tiled=True)  23.6 us
    pallas_call x1, Pallas kernels, partials(): pl.pallas_call(scatter_kernel, grid_spec=pltpu.PrefetchScalarGridSpec(num...  19.8 us
    pallas_call x1, Pallas kernels, merged(): pl.pallas_call(merge_kernel, grid=(STEPS,), in_specs=[pl.BlockSpec((GROUP...  10.3 us
    all_to_all x1, waiting for transfers between devices, shards(): both = lax.all_to_all(spread, 'nodes', 0, 0, tiled=True).reshape(2 * D, D)  6.68 us
    pallas_call x1, Pallas kernels, feature_gradient(): pl.pallas_call(feature_kernel, grid=(BLK_DEV // 2,), in_specs=[whole(OWNE...  6.55 us
    all_to_all x1, starting transfers between devices, shards(): both = lax.all_to_all(spread, 'nodes', 0, 0, tiled=True).reshape(2 * D, D)  5.64 us
  transfers between devices with their start and end apart: 1, of which 1 were waited for; matrix products, arithmetic and copies ran while one was open for 0% of the time, Pallas kernels for 3%

profile of v6, /device:TPU:1, one launch (start us, length us, event | category | flops | bytes accessed | tf_op | source)
XLA Modules:
  0.0 228.2 jit_solution(9788880713431121077)
XLA Ops:
  0.6 0.7 add_convert_fusion
  1.3 0.1 tile.11
  1.4 0.6 pad.5.tag_ref
  2.0 19.8 %shard_map.112 = (f32[8,512,128]{2,1,0:T(8,128)}, f32[512,512]{1,0:T(8,128)}, bf16[128,272,128]{2,1,0:T(8,128)(2,1)}) custom-call(s32[8,10]{1,0:T(8,128)} %col_ref.1, s32[8,10,128,128]{3,2,1,0:T(8,128)} %counts_ref.1, f32[1024,512]{1,0:T(8,128)} %preact_ref.3, f32[1024,512]{1,0:T(8,128)} %cot_ref.3, bf16[1024,512]{1,0:T(8,128)(2,1)} %feat_ref.3, ...), custom_call_target="tpu_custom_call" | custom-call | flops 2684354560 | bytes 23068672 | tf_op jit(solution)/shard_map/pallas_call | solution.py:98
  21.8 116.8 %all_to_all.20.recv_ref = bf16[128,272,128]{2,1,0:T(8,128)(2,1)S(1)} all-to-all(bf16[128,272,128]{2,1,0:T(8,128)(2,1)} %get-tuple-element.8), channel_id=1, replica_groups=mesh['nodes'=128] {'nodes'}, dimensions={0} | all-to-all | bytes 17825792 | tf_op jit(solution)/shard_map/all_to_all | solution.py:275
  138.6 0.0 copy-start.1
  138.6 10.3 %shard_map.113 = bf16[1024,512]{1,0:T(8,128)(2,1)S(1)} custom-call(bf16[128,272,128]{2,1,0:T(8,128)(2,1)S(1)} %all_to_all.20.recv_ref), custom_call_target="tpu_custom_call" | custom-call | flops 8589934592 | bytes 10485760 | tf_op jit(solution)/shard_map/pallas_call | solution.py:159
  148.9 0.0 copy-start
  148.9 0.0 copy-start.4
  148.9 25.7 %all_to_all.21.recv_ref = bf16[128,8,512]{2,1,0:T(8,128)(2,1)S(1)} all-to-all(bf16[128,8,512]{2,1,0:T(8,128)(2,1)S(1)} %bitcast.7), channel_id=1, replica_groups=mesh['nodes'=128] {'nodes'}, dimensions={0} | all-to-all | bytes 2097152 | tf_op jit(solution)/shard_map/all_to_all | solution.py:277
  174.6 0.0 copy-done.1
  174.6 0.0 copy-done
  174.6 0.0 copy-done.4
  174.7 1.4 shard_map.114
  176.1 23.6 %all_to_all.22.shares_ref = bf16[128,8,512]{2,1,0:T(8,128)(2,1)S(1)} all-to-all(bf16[128,8,512]{2,1,0:T(8,128)(2,1)S(1)} %bitcast.6), channel_id=1, replica_groups=mesh['nodes'=128] {'nodes'}, dimensions={0} | all-to-all | bytes 2097152 | tf_op jit(solution)/shard_map/all_to_all | solution.py:281
  199.7 1.2 shard_map.115
  200.9 5.6 %all-to-all-start.3 = ((bf16[128,8,512]{2,1,0:T(8,128)(2,1)}), bf16[128,8,512]{2,1,0:T(8,128)(2,1)}, u32[]{:S(2)}, u32[]{:S(2)}) async-start(bf16[128,8,512]{2,1,0:T(8,128)(2,1)} %shard_map.115), calls=%async_computation.3 | async-start | bytes 2097152 | tf_op jit(solution)/shard_map/all_to_all | solution.py:283
  206.5 0.0 copy-start.2
  206.5 1.6 copy-done.2
  208.1 0.0 copy-start.3
  208.1 1.6 copy-done.3
  209.7 0.0 copy-start.5
  209.7 1.2 copy-done.5
  210.9 0.0 copy-start.6
  210.9 1.2 copy-done.6
  212.2 6.5 %shard_map.116 = f32[1024,512]{1,0:T(8,128)} custom-call(bf16[128,8,512]{2,1,0:T(8,128)(2,1)S(1)} %all_to_all.21.recv_ref, f32[8,512,128]{2,1,0:T(8,128)S(1)} %copy-done.1, f32[1024,512]{1,0:T(8,128)S(1)} %copy-done.2, f32[1024,512]{1,0:T(8,128)S(1)} %copy-done.3, f32[512,512]{1,0:T(8,128)S(1)} %copy-done.5, f32[512,512]{1,0:T(8,128)S(1)} %copy-done.6), custom_call_target="tpu_custom_call" | custom-call | flops 3221225472 | bytes 10485760 | tf_op jit(solution)/shard_map/pallas_call | solution.py:245
  218.7 6.7 %all-to-all-done.3 = bf16[128,8,512]{2,1,0:T(8,128)(2,1)} async-done(((bf16[128,8,512]{2,1,0:T(8,128)(2,1)}), bf16[128,8,512]{2,1,0:T(8,128)(2,1)}, u32[]{:S(2)}, u32[]{:S(2)}) %all-to-all-start.3) | async-done | bytes 1048608 | tf_op jit(solution)/shard_map/all_to_all | solution.py:283
  225.4 2.8 %multiply_bitcast_fusion = (f32[512,512]{1,0:T(8,128)}, f32[512,512]{1,0:T(8,128)}) fusion(bf16[128,8,512]{2,1,0:T(8,128)(2,1)} %all-to-all-done.3), kind=kLoop, calls=%fused_computation | loop fusion | flops 1048576 | bytes 3145728 | tf_op jit(solution)/shard_map/mul | solution.py:286
  (1 shorter events, 0.0 us)
Async XLA Ops:
  138.6 36.1 %copy-start.1 = (f32[8,512,128]{2,1,0:T(8,128)S(1)}, f32[8,512,128]{2,1,0:T(8,128)}, u32[]{:S(2)}) copy-start(f32[8,512,128]{2,1,0:T(8,128)} %get-tuple-element.9.own_ref) | copy-start | bytes 6291460
  148.9 25.7 %copy-start = (bf16[1024,512]{1,0:T(8,128)(2,1)S(1)}, bf16[1024,512]{1,0:T(8,128)(2,1)}, u32[]{:S(2)}) copy-start(bf16[1024,512]{1,0:T(8,128)(2,1)} %feat_ref.3) | copy-start | bytes 3145732
  148.9 25.7 %copy-start.4 = (f32[512,512]{1,0:T(8,128)S(1)}, f32[512,512]{1,0:T(8,128)}, u32[]{:S(2)}) copy-start(f32[512,512]{1,0:T(8,128)} %get-tuple-element.10.self_ref) | copy-start | bytes 3145732
  200.9 24.5 %all-to-all-start.3 = ((bf16[128,8,512]{2,1,0:T(8,128)(2,1)}), bf16[128,8,512]{2,1,0:T(8,128)(2,1)}, u32[]{:S(2)}, u32[]{:S(2)}) async-start(bf16[128,8,512]{2,1,0:T(8,128)(2,1)} %shard_map.115), calls=%async_computation.3 | async-start | bytes 2097152 | tf_op jit(solution)/shard_map/all_to_all | solution.py:283
  206.5 1.6 copy-start.2
  208.1 1.6 copy-start.3
  209.7 1.2 copy-start.5
  210.9 1.2 copy-start.6

commit v7 on v6

--- a/solution.py
+++ b/solution.py
@@ -18,8 +18,7 @@
 TAG = 16
 PIECES = D // OWNERS
 SENT = PIECES * NB + TAG
-BATCH = 16
-PITCH = D + 8
+PITCH = BLK + 8
 F32 = jnp.float32
 BF16 = jnp.bfloat16
 
@@ -38,7 +37,7 @@
 
 
 def scatter_kernel(
-    col_ref, counts_ref, preact_ref, cot_ref, feat_ref, tag_ref, own_ref, self_ref, send_ref, acc, stage, sems
+    col_ref, counts_ref, preact_ref, cot_ref, feat_ref, tag_ref, own_ref, self_ref, send_ref, acc
 ):
     b = pl.program_id(0)
 
@@ -47,50 +46,34 @@
         acc[...] = jnp.zeros_like(acc)
         self_ref[...] = jnp.zeros_like(self_ref)
 
+    def column(r, c):
+        return pl.ds(pl.multiple_of((r * COLUMNS + c) * PITCH, 8), BLK)
+
     counts = counts_ref[0].astype(F32)
     degree = 1.0 + jnp.sum(jnp.sum(counts, axis=0), axis=1, keepdims=True)
-    root = jnp.broadcast_to(jnp.sqrt(degree), (BLK, BLK)).T[:1]
-    grad = jnp.where(preact_ref[...] > 0, cot_ref[...], 0.0).T
-    both = jnp.concatenate(halves(grad), axis=1)
-    feat = feat_ref[...]
-    self_ref[...] += dot(both, jnp.concatenate([feat, feat], axis=0))
-    both = jnp.concatenate(halves(grad / root), axis=1)
-    tiles = counts.astype(BF16)
-
-    def column(c):
-        return pl.ds(pl.multiple_of(c * PITCH, 8), D)
-
+    grad = jnp.where(preact_ref[...] > 0, cot_ref[...], 0.0)
+    feat = feat_ref[...].astype(F32).T.astype(BF16)
+    self_ref[...] += dot(jnp.concatenate([feat, feat], axis=1), jnp.concatenate(halves(grad), axis=0))
+    both = jnp.concatenate(halves(grad / jnp.sqrt(degree)), axis=0)
     for t in range(0, K, 2):
-        pair = jnp.concatenate([tiles[t], tiles[t + 1]], axis=1)
-        part = dot(both, jnp.concatenate([pair, pair], axis=0))
-        acc[column(col_ref[b, t])] += part[:, :BLK]
-        acc[column(col_ref[b, t + 1])] += part[:, BLK:]
+        pair = jnp.concatenate([counts[t].T, counts[t + 1].T], axis=0).astype(BF16)
+        part = dot(jnp.concatenate([pair, pair], axis=1), both)
+        for i in range(2):
+            for r in range(PIECES):
+                acc[column(r, col_ref[b, t + i])] += part[i * BLK : (i + 1) * BLK, r * BLK : (r + 1) * BLK]
 
     @pl.when(b == BLK_DEV - 1)
     def _():
-        def put(g):
-            rows = pl.ds(g * BATCH, BATCH)
-            return pltpu.make_async_copy(stage.at[rows], send_ref.at[rows], sems.at[g])
-
-        @pl.loop(0, OWNERS // BATCH)
-        def _(g):
-            @pl.loop(0, BATCH)
-            def _(i):
-                j = g * BATCH + i
-                for r in range(PIECES):
-                    start = BLK_DEV * PITCH + r * OWNERS + j
-                    stage[j, r * NB : (r + 1) * NB] = acc[pl.ds(start, NB, stride=PITCH)].astype(BF16)
-                stage[j, PIECES * NB :] = tag_ref[...]
-
-            put(g).start()
+        @pl.loop(0, OWNERS)
+        def _(j):
+            for r in range(PIECES):
+                start = (r * COLUMNS + BLK_DEV) * PITCH + j
+                send_ref[j, r * NB : (r + 1) * NB] = acc[pl.ds(start, NB, stride=PITCH)].astype(BF16)
+            send_ref[j, PIECES * NB :] = tag_ref[...]
 
         for c in range(BLK_DEV):
-            own_ref[c] = acc[c * PITCH : c * PITCH + D]
-        self_ref[...] = self_ref[...].T
-
-        @pl.loop(0, OWNERS // BATCH)
-        def _(g):
-            put(g).wait()
+            for r in range(PIECES):
+                own_ref[c * BLK : (c + 1) * BLK, r * BLK : (r + 1) * BLK] = acc[column(r, c)]
 
 
 def partials(tile_col, counts, preact, cotangent, features, tag):
@@ -107,26 +90,24 @@
                 rows,
                 whole(TAG, BLK),
             ],
-            out_specs=[whole(BLK_DEV, D, BLK), whole(D, D), pl.BlockSpec(memory_space=pl.ANY)],
+            out_specs=[whole(BLK_DEV * BLK, D), whole(D, D), pl.BlockSpec(memory_space=pltpu.VMEM)],
             scratch_shapes=[
-                pltpu.VMEM((COLUMNS * PITCH, BLK), F32),
-                pltpu.VMEM((OWNERS, SENT, BLK), BF16),
-                pltpu.SemaphoreType.DMA((OWNERS // BATCH,)),
+                pltpu.VMEM((PIECES * COLUMNS * PITCH, BLK), F32),
             ],
         ),
         out_shape=[
-            jax.ShapeDtypeStruct((BLK_DEV, D, BLK), F32),
-            jax.ShapeDtypeStruct((D, D), F32),
-            jax.ShapeDtypeStruct((OWNERS, SENT, BLK), BF16),
+            pltpu.VMEM((BLK_DEV * BLK, D), F32),
+            pltpu.VMEM((D, D), F32),
+            pltpu.VMEM((OWNERS, SENT, BLK), BF16),
         ],
-        compiler_params=pltpu.CompilerParams(vmem_limit_bytes=58 << 20),
+        compiler_params=pltpu.CompilerParams(vmem_limit_bytes=50 << 20),
         cost_estimate=pl.CostEstimate(
             flops=4 * BLK_DEV * K * BLK * BLK * D, bytes_accessed=22 << 20, transcendentals=0
         ),
     )(tile_col, counts, preact, cotangent, features, tag)
 
 
-GROUP = 16
+GROUP = 32
 STEPS = OWNERS // GROUP
 BINS = OWNERS * BLK_DEV
 MERGED = 256
@@ -171,28 +152,28 @@
 
 
 def add_own(recv_ref, own_ref, flat, total):
-    arrived = recv_ref[...].astype(F32).reshape(BINS, PIECES * BLK)
+    arrived = recv_ref[...].astype(F32).reshape(BINS, D)
     for r in range(PIECES):
         flat[r * BINS : (r + 1) * BINS] = arrived[:, r * BLK : (r + 1) * BLK]
     for g in range(BLK_DEV):
         for r in range(PIECES):
-            rows = slice(r * OWNERS, (r + 1) * OWNERS)
-            total[g, rows] = own_ref[g, rows] + flat[pl.ds(r * BINS + g, OWNERS, stride=BLK_DEV)]
+            place = slice(g * BLK, (g + 1) * BLK), slice(r * BLK, (r + 1) * BLK)
+            total[place] = own_ref[place] + flat[pl.ds(r * BINS + g, OWNERS, stride=BLK_DEV)]
 
 
 def neigh_kernel(recv_ref, own_ref, feat_ref, self_ref, joined_ref, flat, total):
     add_own(recv_ref, own_ref, flat, total)
     neigh = jnp.zeros((D, D), F32)
-    for g in range(0, BLK_DEV, 2):
-        upper, lower = halves(jnp.concatenate([total[g], total[g + 1]], axis=1))
-        feat = feat_ref[g * BLK : (g + 2) * BLK, :]
-        neigh += dot(upper, feat) + dot(lower, feat)
+    for g in range(0, BLK_DEV * BLK, 2 * BLK):
+        upper, lower = halves(total[g : g + 2 * BLK])
+        feat = feat_ref[g : g + 2 * BLK].astype(F32).T.astype(BF16)
+        neigh += dot(feat, upper) + dot(feat, lower)
     joined_ref[:D] = self_ref[...].astype(BF16)
-    joined_ref[D:] = neigh.T.astype(BF16)
+    joined_ref[D:] = neigh.astype(BF16)
 
 
 VMEM_SPEC = pl.BlockSpec(memory_space=pltpu.VMEM)
-TOTAL_SCRATCH = [pltpu.VMEM((PIECES * BINS, BLK), F32), pltpu.VMEM((BLK_DEV, D, BLK), F32)]
+TOTAL_SCRATCH = [pltpu.VMEM((PIECES * BINS, BLK), F32), pltpu.VMEM((BLK_DEV * BLK, D), F32)]
 
 
 def weight_gradients(received, own, features, self_part):
@@ -235,7 +216,7 @@
     upper, lower = halves(grad)
     w_upper, w_lower = halves(self_ref[...].T)
     result = dot(upper, w_upper) + dot(lower, w_upper) + dot(upper, w_lower)
-    upper, lower = halves(jnp.concatenate([total[2 * g], total[2 * g + 1]], axis=1).T)
+    upper, lower = halves(total[pl.ds(pl.multiple_of(2 * BLK * g, BLK), 2 * BLK)])
     w_upper, w_lower = halves(neigh_ref[...].T)
     grad_ref[...] = result + (dot(upper, w_upper) + dot(lower, w_upper) + dot(upper, w_lower))
 
@@ -247,7 +228,7 @@
         grid=(BLK_DEV // 2,),
         in_specs=[
             whole(OWNERS, BLK_DEV, PIECES * BLK),
-            whole(BLK_DEV, D, BLK),
+            whole(BLK_DEV * BLK, D),
             rows,
             rows,
             whole(D, D),
@@ -256,7 +237,7 @@
         out_specs=rows,
         out_shape=jax.ShapeDtypeStruct((BLK_DEV * BLK, D), F32),
         scratch_shapes=TOTAL_SCRATCH,
-        compiler_params=pltpu.CompilerParams(vmem_limit_bytes=32 << 20),
+        compiler_params=pltpu.CompilerParams(vmem_limit_bytes=20 << 20),
         cost_estimate=pl.CostEstimate(
             flops=12 * BLK_DEV * BLK * D * D, bytes_accessed=10 << 20, transcendentals=0
         ),

time: 229 us -> 225 us (0.983)
  Pallas kernels: 39.3 us -> 35.9 us
    pallas_call x1, Pallas kernels: 19.8 us -> 16.8 us  [partials(): pl.pallas_call(scatter_kernel, grid_spec=pltpu.PrefetchScalarGridSpec(num...]
    unnamed x14 -> x10, local copies, waits for them, and re-layouts: 5.64 us -> 5.63 us
where the time goes in v7:
time: 225 us; the launch traced here: 224 us
  blocking collectives  166 us (74%)
  Pallas kernels  35.9 us (16%)
  waiting for transfers between devices  6.63 us (3%)
  local copies, waits for them, and re-layouts  6.32 us (3%)
  starting transfers between devices  5.64 us (3%)
  other arithmetic  3.49 us (2%)
    all_to_all x1, blocking collectives, shards(): received = lax.all_to_all(outgoing, 'nodes', 0, 0, tiled=True)  116 us
    all_to_all x1, blocking collectives, shards(): sums = lax.all_to_all(sums, 'nodes', 0, 0, tiled=True)  25.8 us
    all_to_all x1, blocking collectives, shards(): lax.all_to_all(joined.reshape(OWNERS, rows, D), 'nodes', 0, 0, tiled=True)  23.6 us
    pallas_call x1, Pallas kernels, partials(): pl.pallas_call(scatter_kernel, grid_spec=pltpu.PrefetchScalarGridSpec(num...  16.8 us
    pallas_call x1, Pallas kernels, merged(): pl.pallas_call(merge_kernel, grid=(STEPS,), in_specs=[pl.BlockSpec((GROUP...  9.59 us
    all_to_all x1, waiting for transfers between devices, shards(): both = lax.all_to_all(spread, 'nodes', 0, 0, tiled=True).reshape(2 * D, D)  6.63 us
    pallas_call x1, Pallas kernels, feature_gradient(): pl.pallas_call(feature_kernel, grid=(BLK_DEV // 2,), in_specs=[whole(OWNE...  6.59 us
    all_to_all x1, starting transfers between devices, shards(): both = lax.all_to_all(spread, 'nodes', 0, 0, tiled=True).reshape(2 * D, D)  5.64 us
  transfers between devices with their start and end apart: 1, of which 1 were waited for; matrix products, arithmetic and copies ran while one was open for 0% of the time, Pallas kernels for 3%

profile of v7, /device:TPU:1, one launch (start us, length us, event | category | flops | bytes accessed | tf_op | source)
XLA Modules:
  0.0 224.4 jit_solution(1759502809195029700)
XLA Ops:
  0.6 0.7 add_convert_fusion
  1.3 0.1 tile.11
  1.4 0.6 pad.5.tag_ref
  2.0 16.8 %shard_map.112 = (f32[1024,512]{1,0:T(8,128)S(1)}, f32[512,512]{1,0:T(8,128)S(1)}, bf16[128,272,128]{2,1,0:T(8,128)(2,1)S(1)}) custom-call(s32[8,10]{1,0:T(8,128)} %col_ref.1, s32[8,10,128,128]{3,2,1,0:T(8,128)} %counts_ref.1, f32[1024,512]{1,0:T(8,128)} %preact_ref.3, f32[1024,512]{1,0:T(8,128)} %cot_ref.3, bf16[1024,512]{1,0:T(8,128)(2,1)} %feat_ref.3, ...), custom_call_target="tpu_custom_call" | custom-call | flops 2684354560 | bytes 23068672 | tf_op jit(solution)/shard_map/pallas_call | solution.py:81
  18.8 116.4 %all_to_all.20.recv_ref = bf16[128,272,128]{2,1,0:T(8,128)(2,1)S(1)} all-to-all(bf16[128,272,128]{2,1,0:T(8,128)(2,1)S(1)} %get-tuple-element.8), channel_id=1, replica_groups=mesh['nodes'=128] {'nodes'}, dimensions={0} | all-to-all | bytes 17825792 | tf_op jit(solution)/shard_map/all_to_all | solution.py:256
  135.2 9.6 %shard_map.113 = bf16[1024,512]{1,0:T(8,128)(2,1)S(1)} custom-call(bf16[128,272,128]{2,1,0:T(8,128)(2,1)S(1)} %all_to_all.20.recv_ref), custom_call_target="tpu_custom_call" | custom-call | flops 8589934592 | bytes 10485760 | tf_op jit(solution)/shard_map/pallas_call | solution.py:140
  144.8 0.0 copy-start
  144.8 25.8 %all_to_all.21.recv_ref = bf16[128,8,512]{2,1,0:T(8,128)(2,1)S(1)} all-to-all(bf16[128,8,512]{2,1,0:T(8,128)(2,1)S(1)} %bitcast.7), channel_id=1, replica_groups=mesh['nodes'=128] {'nodes'}, dimensions={0} | all-to-all | bytes 2097152 | tf_op jit(solution)/shard_map/all_to_all | solution.py:258
  170.7 0.0 copy-done
  170.7 1.7 shard_map.114
  172.4 23.6 %all_to_all.22.shares_ref = bf16[128,8,512]{2,1,0:T(8,128)(2,1)S(1)} all-to-all(bf16[128,8,512]{2,1,0:T(8,128)(2,1)S(1)} %bitcast.6), channel_id=1, replica_groups=mesh['nodes'=128] {'nodes'}, dimensions={0} | all-to-all | bytes 2097152 | tf_op jit(solution)/shard_map/all_to_all | solution.py:262
  195.9 1.2 shard_map.115
  197.1 5.6 %all-to-all-start.3 = ((bf16[128,8,512]{2,1,0:T(8,128)(2,1)}), bf16[128,8,512]{2,1,0:T(8,128)(2,1)}, u32[]{:S(2)}, u32[]{:S(2)}) async-start(bf16[128,8,512]{2,1,0:T(8,128)(2,1)} %shard_map.115), calls=%async_computation.3 | async-start | bytes 2097152 | tf_op jit(solution)/shard_map/all_to_all | solution.py:264
  202.8 0.0 copy-start.1
  202.8 1.6 copy-done.1
  204.4 0.0 copy-start.2
  204.4 1.6 copy-done.2
  206.0 0.0 copy-start.3
  206.0 1.2 copy-done.3
  207.2 0.0 copy-start.4
  207.2 1.2 copy-done.4
  208.4 6.6 %shard_map.116 = f32[1024,512]{1,0:T(8,128)} custom-call(bf16[128,8,512]{2,1,0:T(8,128)(2,1)S(1)} %all_to_all.21.recv_ref, f32[1024,512]{1,0:T(8,128)S(1)} %get-tuple-element.9.own_ref, f32[1024,512]{1,0:T(8,128)S(1)} %copy-done.1, f32[1024,512]{1,0:T(8,128)S(1)} %copy-done.2, f32[512,512]{1,0:T(8,128)S(1)} %copy-done.3, f32[512,512]{1,0:T(8,128)S(1)} %copy-done.4), custom_call_target="tpu_custom_call" | custom-call | flops 3221225472 | bytes 10485760 | tf_op jit(solution)/shard_map/pallas_call | solution.py:226
  215.0 6.6 %all-to-all-done.3 = bf16[128,8,512]{2,1,0:T(8,128)(2,1)} async-done(((bf16[128,8,512]{2,1,0:T(8,128)(2,1)}), bf16[128,8,512]{2,1,0:T(8,128)(2,1)}, u32[]{:S(2)}, u32[]{:S(2)}) %all-to-all-start.3) | async-done | bytes 1048608 | tf_op jit(solution)/shard_map/all_to_all | solution.py:264
  221.6 2.8 %multiply_bitcast_fusion = (f32[512,512]{1,0:T(8,128)}, f32[512,512]{1,0:T(8,128)}) fusion(bf16[128,8,512]{2,1,0:T(8,128)(2,1)} %all-to-all-done.3), kind=kLoop, calls=%fused_computation | loop fusion | flops 1048576 | bytes 3145728 | tf_op jit(solution)/shard_map/mul | solution.py:267
  (1 shorter events, 0.0 us)
Async XLA Ops:
  144.8 25.8 %copy-start = (bf16[1024,512]{1,0:T(8,128)(2,1)S(1)}, bf16[1024,512]{1,0:T(8,128)(2,1)}, u32[]{:S(2)}) copy-start(bf16[1024,512]{1,0:T(8,128)(2,1)} %feat_ref.3) | copy-start | bytes 3145732
  197.1 24.5 %all-to-all-start.3 = ((bf16[128,8,512]{2,1,0:T(8,128)(2,1)}), bf16[128,8,512]{2,1,0:T(8,128)(2,1)}, u32[]{:S(2)}, u32[]{:S(2)}) async-start(bf16[128,8,512]{2,1,0:T(8,128)(2,1)} %shard_map.115), calls=%async_computation.3 | async-start | bytes 2097152 | tf_op jit(solution)/shard_map/all_to_all | solution.py:264
  202.8 1.6 copy-start.1
  204.4 1.6 copy-start.2
  206.0 1.2 copy-start.3
  207.2 1.2 copy-start.4

commit v8 on v7

--- a/solution.py
+++ b/solution.py
@@ -258,11 +258,12 @@
     sums = lax.all_to_all(sums, "nodes", 0, 0, tiled=True)
     joined = weight_gradients(sums, own, features, self_part)
 
+    joined, sums = lax.optimization_barrier((joined, sums))
     rows = 2 * D // OWNERS
     shares = lax.all_to_all(joined.reshape(OWNERS, rows, D), "nodes", 0, 0, tiled=True)
-    spread, sums = lax.optimization_barrier((added_up(shares), sums))
+    grad_features = feature_gradient(sums, own, preact, cotangent, w_self, w_neigh)
+    spread, grad_features = lax.optimization_barrier((added_up(shares), grad_features))
     both = lax.all_to_all(spread, "nodes", 0, 0, tiled=True).reshape(2 * D, D)
-    grad_features = feature_gradient(sums, own, preact, cotangent, w_self, w_neigh)
     scale = 1.0 / math.sqrt(OWNERS * BLK_DEV * BLK)
     return grad_features, both[:D].astype(F32) * scale, both[D:].astype(F32) * scale
 

time: 225 us -> 223 us (level)
    unnamed x10 -> x14, local copies, waits for them, and re-layouts: 5.63 us -> 6.01 us
where the time goes in v8:
time: 223 us
  blocking collectives  166 us (74%)
  Pallas kernels  35.9 us (16%)
  local copies, waits for them, and re-layouts  6.7 us (3%)
  waiting for transfers between devices  6.6 us (3%)
  starting transfers between devices  4.73 us (2%)
  other arithmetic  2.3 us (1%)
    all_to_all x1, blocking collectives, shards(): received = lax.all_to_all(outgoing, 'nodes', 0, 0, tiled=True)  116 us
    all_to_all x1, blocking collectives, shards(): sums = lax.all_to_all(sums, 'nodes', 0, 0, tiled=True)  25.8 us
    all_to_all x1, blocking collectives, shards(): both = lax.all_to_all(spread, 'nodes', 0, 0, tiled=True).reshape(2 * D, D)  23.6 us
    pallas_call x1, Pallas kernels, partials(): pl.pallas_call(scatter_kernel, grid_spec=pltpu.PrefetchScalarGridSpec(num...  16.8 us
    pallas_call x1, Pallas kernels, merged(): pl.pallas_call(merge_kernel, grid=(STEPS,), in_specs=[pl.BlockSpec((GROUP...  9.59 us
    all_to_all x1, waiting for transfers between devices, shards(): lax.all_to_all(joined.reshape(OWNERS, rows, D), 'nodes', 0, 0, tiled=True)  6.6 us
    pallas_call x1, Pallas kernels, feature_gradient(): pl.pallas_call(feature_kernel, grid=(BLK_DEV // 2,), in_specs=[whole(OWNE...  6.59 us
    unnamed x14, local copies, waits for them, and re-layouts  6.01 us
  transfers between devices with their start and end apart: 1, of which 1 were waited for; matrix products, arithmetic and copies ran while one was open for 0% of the time, Pallas kernels for 3%

profile of v8, /device:TPU:1, one launch (start us, length us, event | category | flops | bytes accessed | tf_op | source)
XLA Modules:
  0.0 222.7 jit_solution(1516602124357294211)
XLA Ops:
  0.6 0.7 add_convert_fusion
  1.3 0.1 tile.11
  1.4 0.6 pad.5.tag_ref
  2.0 16.8 %shard_map.112 = (f32[1024,512]{1,0:T(8,128)S(1)}, f32[512,512]{1,0:T(8,128)S(1)}, bf16[128,272,128]{2,1,0:T(8,128)(2,1)S(1)}) custom-call(s32[8,10]{1,0:T(8,128)} %col_ref.1, s32[8,10,128,128]{3,2,1,0:T(8,128)} %counts_ref.1, f32[1024,512]{1,0:T(8,128)} %preact_ref.3, f32[1024,512]{1,0:T(8,128)} %cot_ref.3, bf16[1024,512]{1,0:T(8,128)(2,1)} %feat_ref.3, ...), custom_call_target="tpu_custom_call" | custom-call | flops 2684354560 | bytes 23068672 | tf_op jit(solution)/shard_map/pallas_call | solution.py:81
  18.8 0.0 copy-start.1
  18.8 116.4 %all_to_all.20.recv_ref = bf16[128,272,128]{2,1,0:T(8,128)(2,1)S(1)} all-to-all(bf16[128,272,128]{2,1,0:T(8,128)(2,1)S(1)} %get-tuple-element.10), channel_id=1, replica_groups=mesh['nodes'=128] {'nodes'}, dimensions={0} | all-to-all | bytes 17825792 | tf_op jit(solution)/shard_map/all_to_all | solution.py:256
  135.3 9.6 %shard_map.113 = bf16[1024,512]{1,0:T(8,128)(2,1)S(1)} custom-call(bf16[128,272,128]{2,1,0:T(8,128)(2,1)S(1)} %all_to_all.20.recv_ref), custom_call_target="tpu_custom_call" | custom-call | flops 8589934592 | bytes 10485760 | tf_op jit(solution)/shard_map/pallas_call | solution.py:140
  144.9 0.0 copy-start
  144.9 25.8 %all_to_all.21.recv_ref = bf16[128,8,512]{2,1,0:T(8,128)(2,1)S(1)} all-to-all(bf16[128,8,512]{2,1,0:T(8,128)(2,1)S(1)} %bitcast.6), channel_id=1, replica_groups=mesh['nodes'=128] {'nodes'}, dimensions={0} | all-to-all | bytes 2097152 | tf_op jit(solution)/shard_map/all_to_all | solution.py:258
  170.7 0.0 copy-done.1
  170.7 0.0 copy-done
  170.7 2.6 %shard_map.114 = bf16[1024,512]{1,0:T(8,128)(2,1)} custom-call(bf16[128,8,512]{2,1,0:T(8,128)(2,1)S(1)} %all_to_all.21.recv_ref, f32[1024,512]{1,0:T(8,128)S(1)} %get-tuple-element.11.own_ref, bf16[1024,512]{1,0:T(8,128)(2,1)S(1)} %copy-done, f32[512,512]{1,0:T(8,128)S(1)} %get-tuple-element.12.self_ref), custom_call_target="tpu_custom_call" | custom-call | flops 1073741824 | bytes 6291456 | tf_op jit(solution)/shard_map/pallas_call | solution.py:180
  173.4 0.0 copy-start.5
  173.4 4.7 %all-to-all-start.2 = ((bf16[128,8,512]{2,1,0:T(8,128)(2,1)}), bf16[128,8,512]{2,1,0:T(8,128)(2,1)S(1)}, u32[]{:S(2)}, u32[]{:S(2)}) async-start(bf16[128,8,512]{2,1,0:T(8,128)(2,1)} %bitcast.1), calls=%async_computation.2 | async-start | bytes 2097152 | tf_op jit(solution)/shard_map/all_to_all | solution.py:263
  178.1 0.0 copy-done.5
  178.1 0.0 copy-start.2
  178.1 1.6 copy-done.2
  179.7 0.0 copy-start.3
  179.7 1.6 copy-done.3
  181.3 0.0 copy-start.4
  181.3 1.6 copy-done.4
  182.9 0.0 copy-start.6
  182.9 1.2 copy-done.6
  184.1 6.6 %shard_map.116 = f32[1024,512]{1,0:T(8,128)} custom-call(bf16[128,8,512]{2,1,0:T(8,128)(2,1)S(1)} %all_to_all.21.recv_ref, f32[1024,512]{1,0:T(8,128)S(1)} %copy-done.2, f32[1024,512]{1,0:T(8,128)S(1)} %copy-done.3, f32[1024,512]{1,0:T(8,128)S(1)} %copy-done.4, f32[512,512]{1,0:T(8,128)S(1)} %copy-done.5, f32[512,512]{1,0:T(8,128)S(1)} %copy-done.6), custom_call_target="tpu_custom_call" | custom-call | flops 3221225472 | bytes 10485760 | tf_op jit(solution)/shard_map/pallas_call | solution.py:226
  190.7 6.6 %all-to-all-done.2.shares_ref = bf16[128,8,512]{2,1,0:T(8,128)(2,1)S(1)} async-done(((bf16[128,8,512]{2,1,0:T(8,128)(2,1)}), bf16[128,8,512]{2,1,0:T(8,128)(2,1)S(1)}, u32[]{:S(2)}, u32[]{:S(2)}) %all-to-all-start.2) | async-done | bytes 1048608 | tf_op jit(solution)/shard_map/all_to_all | solution.py:263
  197.3 0.2 shard_map.115
  197.6 23.6 %all_to_all.22 = bf16[128,8,512]{2,1,0:T(8,128)(2,1)S(1)} all-to-all(bf16[128,8,512]{2,1,0:T(8,128)(2,1)S(1)} %shard_map.115), channel_id=1, replica_groups=mesh['nodes'=128] {'nodes'}, dimensions={0} | all-to-all | bytes 2097152 | tf_op jit(solution)/shard_map/all_to_all | solution.py:266
  221.1 1.6 multiply_bitcast_fusion
  (1 shorter events, 0.0 us)
Async XLA Ops:
  18.8 151.9 %copy-start.1 = (f32[1024,512]{1,0:T(8,128)}, f32[1024,512]{1,0:T(8,128)S(1)}, u32[]{:S(2)}) copy-start(f32[1024,512]{1,0:T(8,128)S(1)} %get-tuple-element.11.own_ref) | copy-start | bytes 6291460
  144.9 25.8 %copy-start = (bf16[1024,512]{1,0:T(8,128)(2,1)S(1)}, bf16[1024,512]{1,0:T(8,128)(2,1)}, u32[]{:S(2)}) copy-start(bf16[1024,512]{1,0:T(8,128)(2,1)} %feat_ref.3) | copy-start | bytes 3145732
  173.4 4.7 %copy-start.5 = (f32[512,512]{1,0:T(8,128)S(1)}, f32[512,512]{1,0:T(8,128)}, u32[]{:S(2)}) copy-start(f32[512,512]{1,0:T(8,128)} %self_ref.1) | copy-start | bytes 3145732
  173.4 23.9 %all-to-all-start.2 = ((bf16[128,8,512]{2,1,0:T(8,128)(2,1)}), bf16[128,8,512]{2,1,0:T(8,128)(2,1)S(1)}, u32[]{:S(2)}, u32[]{:S(2)}) async-start(bf16[128,8,512]{2,1,0:T(8,128)(2,1)} %bitcast.1), calls=%async_computation.2 | async-start | bytes 2097152 | tf_op jit(solution)/shard_map/all_to_all | solution.py:263
  178.1 1.6 copy-start.2
  179.7 1.6 copy-start.3
  181.3 1.6 copy-start.4
  182.9 1.2 copy-start.6

commit v9 on v8

--- a/solution.py
+++ b/solution.py
@@ -37,14 +37,19 @@
 
 
 def scatter_kernel(
-    col_ref, counts_ref, preact_ref, cot_ref, feat_ref, tag_ref, own_ref, self_ref, send_ref, acc
+    col_ref, counts_ref, preact_ref, cot_ref, feat_ref, owner_ref, slot_ref, own_ref, self_ref, send_ref, acc, seen
 ):
     b = pl.program_id(0)
 
     @pl.when(b == 0)
     def _():
-        acc[...] = jnp.zeros_like(acc)
+        for r in range(PIECES):
+            acc[pl.ds(r * COLUMNS * PITCH, BLK_DEV * PITCH)] = jnp.zeros((BLK_DEV * PITCH, BLK), F32)
         self_ref[...] = jnp.zeros_like(self_ref)
+
+        @pl.loop(0, COLUMNS)
+        def _(c):
+            seen[c] = jnp.where(c < BLK_DEV, 1, 0)
 
     def column(r, c):
         return pl.ds(pl.multiple_of((r * COLUMNS + c) * PITCH, 8), BLK)
@@ -59,24 +64,33 @@
         pair = jnp.concatenate([counts[t].T, counts[t + 1].T], axis=0).astype(BF16)
         part = dot(jnp.concatenate([pair, pair], axis=1), both)
         for i in range(2):
+            c = col_ref[b, t + i]
+            started = seen[c] > 0
+            seen[c] = 1
             for r in range(PIECES):
-                acc[column(r, col_ref[b, t + i])] += part[i * BLK : (i + 1) * BLK, r * BLK : (r + 1) * BLK]
+                place = column(r, c)
+                new = part[i * BLK : (i + 1) * BLK, r * BLK : (r + 1) * BLK]
+                acc[place] = jnp.where(started, acc[place], 0.0) + new
 
     @pl.when(b == BLK_DEV - 1)
     def _():
+        row = lax.broadcasted_iota(jnp.int32, (TAG, BLK), 0)
+        owners, slots = (jnp.concatenate([ref[...]] * 2, axis=1) for ref in (owner_ref, slot_ref))
+        tag = jnp.where(row == 0, owners, jnp.where(row == 1, slots, 0)).astype(F32).astype(BF16)
+
         @pl.loop(0, OWNERS)
         def _(j):
             for r in range(PIECES):
                 start = (r * COLUMNS + BLK_DEV) * PITCH + j
                 send_ref[j, r * NB : (r + 1) * NB] = acc[pl.ds(start, NB, stride=PITCH)].astype(BF16)
-            send_ref[j, PIECES * NB :] = tag_ref[...]
+            send_ref[j, PIECES * NB :] = tag
 
         for c in range(BLK_DEV):
             for r in range(PIECES):
                 own_ref[c * BLK : (c + 1) * BLK, r * BLK : (r + 1) * BLK] = acc[column(r, c)]
 
 
-def partials(tile_col, counts, preact, cotangent, features, tag):
+def partials(tile_col, counts, preact, cotangent, features, owner, slot):
     rows = pl.BlockSpec((BLK, D), lambda b, *_: (b, 0))
     return pl.pallas_call(
         scatter_kernel,
@@ -88,11 +102,13 @@
                 rows,
                 rows,
                 rows,
-                whole(TAG, BLK),
+                whole(1, NB),
+                whole(1, NB),
             ],
             out_specs=[whole(BLK_DEV * BLK, D), whole(D, D), pl.BlockSpec(memory_space=pltpu.VMEM)],
             scratch_shapes=[
-                pltpu.VMEM((PIECES * COLUMNS * PITCH, BLK), F32),
+                pltpu.VMEM(((PIECES * COLUMNS + 1) * PITCH, BLK), F32),
+                pltpu.SMEM((COLUMNS,), jnp.int32),
             ],
         ),
         out_shape=[
@@ -104,7 +120,7 @@
         cost_estimate=pl.CostEstimate(
             flops=4 * BLK_DEV * K * BLK * BLK * D, bytes_accessed=22 << 20, transcendentals=0
         ),
-    )(tile_col, counts, preact, cotangent, features, tag)
+    )(tile_col, counts, preact, cotangent, features, owner, slot)
 
 
 GROUP = 32
@@ -173,7 +189,7 @@
 
 
 VMEM_SPEC = pl.BlockSpec(memory_space=pltpu.VMEM)
-TOTAL_SCRATCH = [pltpu.VMEM((PIECES * BINS, BLK), F32), pltpu.VMEM((BLK_DEV * BLK, D), F32)]
+TOTAL_SCRATCH = [pltpu.VMEM((PIECES * BINS + BLK_DEV, BLK), F32), pltpu.VMEM((BLK_DEV * BLK, D), F32)]
 
 
 def weight_gradients(received, own, features, self_part):
@@ -244,15 +260,8 @@
     )(received, own, preact, cotangent, w_self, w_neigh)
 
 
-def list_rows(owner, slot):
-    lists = jnp.concatenate([owner, slot], axis=0)
-    return jnp.pad(jnp.tile(lists, (1, BLK // NB)), ((0, TAG - 2), (0, 0))).astype(BF16)
-
-
 def shards(features, preact, cotangent, w_self, w_neigh, tile_counts, tile_col, owner, slot):
-    own, self_part, outgoing = partials(
-        tile_col, tile_counts, preact, cotangent, features, list_rows(owner, slot)
-    )
+    own, self_part, outgoing = partials(tile_col, tile_counts, preact, cotangent, features, owner, slot)
     received = lax.all_to_all(outgoing, "nodes", 0, 0, tiled=True)
     sums = merged(received).reshape(OWNERS, BLK_DEV, PIECES * BLK)
     sums = lax.all_to_all(sums, "nodes", 0, 0, tiled=True)

time: 223 us -> 221 us (level)
  no operation moved by 1% of the time
where the time goes in v9:
time: 221 us; the launch traced here: 220 us
  blocking collectives  166 us (75%)
  Pallas kernels  35 us (16%)
  waiting for transfers between devices  6.61 us (3%)
  local copies, waits for them, and re-layouts  6.01 us (3%)
  starting transfers between devices  4.72 us (2%)
    all_to_all x1, blocking collectives, shards(): received = lax.all_to_all(outgoing, 'nodes', 0, 0, tiled=True)  116 us
    all_to_all x1, blocking collectives, shards(): sums = lax.all_to_all(sums, 'nodes', 0, 0, tiled=True)  25.8 us
    all_to_all x1, blocking collectives, shards(): both = lax.all_to_all(spread, 'nodes', 0, 0, tiled=True).reshape(2 * D, D)  23.6 us
    pallas_call x1, Pallas kernels, partials(): pl.pallas_call(scatter_kernel, grid_spec=pltpu.PrefetchScalarGridSpec(num...  15.9 us
    pallas_call x1, Pallas kernels, merged(): pl.pallas_call(merge_kernel, grid=(STEPS,), in_specs=[pl.BlockSpec((GROUP...  9.59 us
    all_to_all x1, waiting for transfers between devices, shards(): lax.all_to_all(joined.reshape(OWNERS, rows, D), 'nodes', 0, 0, tiled=True)  6.61 us
    pallas_call x1, Pallas kernels, feature_gradient(): pl.pallas_call(feature_kernel, grid=(BLK_DEV // 2,), in_specs=[whole(OWNE...  6.59 us
    unnamed x14, local copies, waits for them, and re-layouts  6.01 us
  transfers between devices with their start and end apart: 1, of which 1 were waited for; matrix products, arithmetic and copies ran while one was open for 0% of the time, Pallas kernels for 3%

profile of v9, /device:TPU:1, one launch (start us, length us, event | category | flops | bytes accessed | tf_op | source)
XLA Modules:
  0.0 220.4 jit_solution(4515491436806102156)
XLA Ops:
  0.6 15.9 %shard_map.112 = (f32[1024,512]{1,0:T(8,128)S(1)}, f32[512,512]{1,0:T(8,128)S(1)}, bf16[128,272,128]{2,1,0:T(8,128)(2,1)S(1)}) custom-call(s32[8,10]{1,0:T(8,128)} %col_ref.1, s32[8,10,128,128]{3,2,1,0:T(8,128)} %counts_ref.1, f32[1024,512]{1,0:T(8,128)} %preact_ref.3, f32[1024,512]{1,0:T(8,128)} %cot_ref.3, bf16[1024,512]{1,0:T(8,128)(2,1)} %feat_ref.3, ...), custom_call_target="tpu_custom_call" | custom-call | flops 2684354560 | bytes 23068672 | tf_op jit(solution)/shard_map/pallas_call | solution.py:95
  16.5 0.0 copy-start.3
  16.5 116.4 %all_to_all.20.recv_ref = bf16[128,272,128]{2,1,0:T(8,128)(2,1)S(1)} all-to-all(bf16[128,272,128]{2,1,0:T(8,128)(2,1)S(1)} %get-tuple-element.10), channel_id=1, replica_groups=mesh['nodes'=128] {'nodes'}, dimensions={0} | all-to-all | bytes 17825792 | tf_op jit(solution)/shard_map/all_to_all | solution.py:265
  133.0 9.6 %shard_map.113 = bf16[1024,512]{1,0:T(8,128)(2,1)S(1)} custom-call(bf16[128,272,128]{2,1,0:T(8,128)(2,1)S(1)} %all_to_all.20.recv_ref), custom_call_target="tpu_custom_call" | custom-call | flops 8589934592 | bytes 10485760 | tf_op jit(solution)/shard_map/pallas_call | solution.py:156
  142.6 0.0 copy-start
  142.6 25.8 %all_to_all.21.recv_ref = bf16[128,8,512]{2,1,0:T(8,128)(2,1)S(1)} all-to-all(bf16[128,8,512]{2,1,0:T(8,128)(2,1)S(1)} %bitcast.6), channel_id=1, replica_groups=mesh['nodes'=128] {'nodes'}, dimensions={0} | all-to-all | bytes 2097152 | tf_op jit(solution)/shard_map/all_to_all | solution.py:267
  168.4 0.0 copy-done.3
  168.4 0.0 copy-done
  168.4 2.7 %shard_map.114 = bf16[1024,512]{1,0:T(8,128)(2,1)} custom-call(bf16[128,8,512]{2,1,0:T(8,128)(2,1)S(1)} %all_to_all.21.recv_ref, f32[1024,512]{1,0:T(8,128)S(1)} %get-tuple-element.11.own_ref, bf16[1024,512]{1,0:T(8,128)(2,1)S(1)} %copy-done, f32[512,512]{1,0:T(8,128)S(1)} %get-tuple-element.12.self_ref), custom_call_target="tpu_custom_call" | custom-call | flops 1073741824 | bytes 6291456 | tf_op jit(solution)/shard_map/pallas_call | solution.py:196
  171.1 0.0 copy-start.5
  171.1 4.7 %all-to-all-start.2 = ((bf16[128,8,512]{2,1,0:T(8,128)(2,1)}), bf16[128,8,512]{2,1,0:T(8,128)(2,1)S(1)}, u32[]{:S(2)}, u32[]{:S(2)}) async-start(bf16[128,8,512]{2,1,0:T(8,128)(2,1)} %bitcast.1), calls=%async_computation.2 | async-start | bytes 2097152 | tf_op jit(solution)/shard_map/all_to_all | solution.py:272
  175.8 0.0 copy-done.5
  175.8 0.0 copy-start.1
  175.8 1.6 copy-done.1
  177.4 0.0 copy-start.2
  177.4 1.6 copy-done.2
  179.0 0.0 copy-start.4
  179.0 1.6 copy-done.4
  180.6 0.0 copy-start.6
  180.6 1.2 copy-done.6
  181.8 6.6 %shard_map.116 = f32[1024,512]{1,0:T(8,128)} custom-call(bf16[128,8,512]{2,1,0:T(8,128)(2,1)S(1)} %all_to_all.21.recv_ref, f32[1024,512]{1,0:T(8,128)S(1)} %copy-done.4, f32[1024,512]{1,0:T(8,128)S(1)} %copy-done.1, f32[1024,512]{1,0:T(8,128)S(1)} %copy-done.2, f32[512,512]{1,0:T(8,128)S(1)} %copy-done.5, f32[512,512]{1,0:T(8,128)S(1)} %copy-done.6), custom_call_target="tpu_custom_call" | custom-call | flops 3221225472 | bytes 10485760 | tf_op jit(solution)/shard_map/pallas_call | solution.py:242
  188.4 6.6 %all-to-all-done.2.shares_ref = bf16[128,8,512]{2,1,0:T(8,128)(2,1)S(1)} async-done(((bf16[128,8,512]{2,1,0:T(8,128)(2,1)}), bf16[128,8,512]{2,1,0:T(8,128)(2,1)S(1)}, u32[]{:S(2)}, u32[]{:S(2)}) %all-to-all-start.2) | async-done | bytes 1048608 | tf_op jit(solution)/shard_map/all_to_all | solution.py:272
  195.0 0.2 shard_map.115
  195.2 23.6 %all_to_all.22 = bf16[128,8,512]{2,1,0:T(8,128)(2,1)S(1)} all-to-all(bf16[128,8,512]{2,1,0:T(8,128)(2,1)S(1)} %shard_map.115), channel_id=1, replica_groups=mesh['nodes'=128] {'nodes'}, dimensions={0} | all-to-all | bytes 2097152 | tf_op jit(solution)/shard_map/all_to_all | solution.py:275
  218.8 1.6 multiply_bitcast_fusion
Async XLA Ops:
  16.5 151.9 %copy-start.3 = (f32[1024,512]{1,0:T(8,128)}, f32[1024,512]{1,0:T(8,128)S(1)}, u32[]{:S(2)}) copy-start(f32[1024,512]{1,0:T(8,128)S(1)} %get-tuple-element.11.own_ref) | copy-start | bytes 6291460
  142.6 25.8 %copy-start = (bf16[1024,512]{1,0:T(8,128)(2,1)S(1)}, bf16[1024,512]{1,0:T(8,128)(2,1)}, u32[]{:S(2)}) copy-start(bf16[1024,512]{1,0:T(8,128)(2,1)} %feat_ref.3) | copy-start | bytes 3145732
  171.1 4.7 %copy-start.5 = (f32[512,512]{1,0:T(8,128)S(1)}, f32[512,512]{1,0:T(8,128)}, u32[]{:S(2)}) copy-start(f32[512,512]{1,0:T(8,128)} %self_ref.1) | copy-start | bytes 3145732
  171.1 23.9 %all-to-all-start.2 = ((bf16[128,8,512]{2,1,0:T(8,128)(2,1)}), bf16[128,8,512]{2,1,0:T(8,128)(2,1)S(1)}, u32[]{:S(2)}, u32[]{:S(2)}) async-start(bf16[128,8,512]{2,1,0:T(8,128)(2,1)} %bitcast.1), calls=%async_computation.2 | async-start | bytes 2097152 | tf_op jit(solution)/shard_map/all_to_all | solution.py:272
  175.8 1.6 copy-start.1
  177.4 1.6 copy-start.2
  179.0 1.6 copy-start.4
  180.6 1.2 copy-start.6

commit v10 on v9

--- a/solution.py
+++ b/solution.py
@@ -123,7 +123,7 @@
     )(tile_col, counts, preact, cotangent, features, owner, slot)
 
 
-GROUP = 32
+GROUP = 64
 STEPS = OWNERS // GROUP
 BINS = OWNERS * BLK_DEV
 MERGED = 256
@@ -160,7 +160,7 @@
         out_specs=whole(BINS, PIECES * BLK),
         out_shape=jax.ShapeDtypeStruct((BINS, PIECES * BLK), BF16),
         scratch_shapes=[pltpu.VMEM((BINS, PIECES * BLK), F32)],
-        compiler_params=pltpu.CompilerParams(vmem_limit_bytes=24 << 20),
+        compiler_params=pltpu.CompilerParams(vmem_limit_bytes=32 << 20),
         cost_estimate=pl.CostEstimate(
             flops=2 * BINS * OWNERS * NB * PIECES * BLK, bytes_accessed=10 << 20, transcendentals=0
         ),
@@ -199,7 +199,7 @@
         out_specs=VMEM_SPEC,
         out_shape=jax.ShapeDtypeStruct((2 * D, D), BF16),
         scratch_shapes=TOTAL_SCRATCH,
-        compiler_params=pltpu.CompilerParams(vmem_limit_bytes=24 << 20),
+        compiler_params=pltpu.CompilerParams(vmem_limit_bytes=32 << 20),
         cost_estimate=pl.CostEstimate(
             flops=4 * BLK_DEV * BLK * D * D, bytes_accessed=6 << 20, transcendentals=0
         ),

time: 221 us -> 221 us (level)
  no operation moved by 1% of the time
where the time goes in v10:
time: 221 us; the launch traced here: 220 us
  blocking collectives  166 us (75%)
  Pallas kernels  34.6 us (16%)
  waiting for transfers between devices  6.6 us (3%)
  local copies, waits for them, and re-layouts  6.01 us (3%)
  starting transfers between devices  4.73 us (2%)
    all_to_all x1, blocking collectives, shards(): received = lax.all_to_all(outgoing, 'nodes', 0, 0, tiled=True)  116 us
    all_to_all x1, blocking collectives, shards(): sums = lax.all_to_all(sums, 'nodes', 0, 0, tiled=True)  25.8 us
    all_to_all x1, blocking collectives, shards(): both = lax.all_to_all(spread, 'nodes', 0, 0, tiled=True).reshape(2 * D, D)  23.6 us
    pallas_call x1, Pallas kernels, partials(): pl.pallas_call(scatter_kernel, grid_spec=pltpu.PrefetchScalarGridSpec(num...  15.9 us
    pallas_call x1, Pallas kernels, merged(): pl.pallas_call(merge_kernel, grid=(STEPS,), in_specs=[pl.BlockSpec((GROUP...  9.22 us
    all_to_all x1, waiting for transfers between devices, shards(): lax.all_to_all(joined.reshape(OWNERS, rows, D), 'nodes', 0, 0, tiled=True)  6.6 us
    pallas_call x1, Pallas kernels, feature_gradient(): pl.pallas_call(feature_kernel, grid=(BLK_DEV // 2,), in_specs=[whole(OWNE...  6.59 us
    unnamed x14, local copies, waits for them, and re-layouts  6.01 us
  transfers between devices with their start and end apart: 1, of which 1 were waited for; matrix products, arithmetic and copies ran while one was open for 0% of the time, Pallas kernels for 3%

profile of v10, /device:TPU:1, one launch (start us, length us, event | category | flops | bytes accessed | tf_op | source)
XLA Modules:
  0.0 220.1 jit_solution(13430045144336647308)
XLA Ops:
  0.6 15.9 %shard_map.112 = (f32[1024,512]{1,0:T(8,128)S(1)}, f32[512,512]{1,0:T(8,128)S(1)}, bf16[128,272,128]{2,1,0:T(8,128)(2,1)S(1)}) custom-call(s32[8,10]{1,0:T(8,128)} %col_ref.1, s32[8,10,128,128]{3,2,1,0:T(8,128)} %counts_ref.1, f32[1024,512]{1,0:T(8,128)} %preact_ref.3, f32[1024,512]{1,0:T(8,128)} %cot_ref.3, bf16[1024,512]{1,0:T(8,128)(2,1)} %feat_ref.3, ...), custom_call_target="tpu_custom_call" | custom-call | flops 2684354560 | bytes 23068672 | tf_op jit(solution)/shard_map/pallas_call | solution.py:95
  16.5 0.0 copy-start.3
  16.5 116.4 %all_to_all.20.recv_ref = bf16[128,272,128]{2,1,0:T(8,128)(2,1)S(1)} all-to-all(bf16[128,272,128]{2,1,0:T(8,128)(2,1)S(1)} %get-tuple-element.10), channel_id=1, replica_groups=mesh['nodes'=128] {'nodes'}, dimensions={0} | all-to-all | bytes 17825792 | tf_op jit(solution)/shard_map/all_to_all | solution.py:265
  133.0 9.2 %shard_map.113 = bf16[1024,512]{1,0:T(8,128)(2,1)S(1)} custom-call(bf16[128,272,128]{2,1,0:T(8,128)(2,1)S(1)} %all_to_all.20.recv_ref), custom_call_target="tpu_custom_call" | custom-call | flops 8589934592 | bytes 10485760 | tf_op jit(solution)/shard_map/pallas_call | solution.py:156
  142.2 0.0 copy-start
  142.2 25.8 %all_to_all.21.recv_ref = bf16[128,8,512]{2,1,0:T(8,128)(2,1)S(1)} all-to-all(bf16[128,8,512]{2,1,0:T(8,128)(2,1)S(1)} %bitcast.6), channel_id=1, replica_groups=mesh['nodes'=128] {'nodes'}, dimensions={0} | all-to-all | bytes 2097152 | tf_op jit(solution)/shard_map/all_to_all | solution.py:267
  168.0 0.0 copy-done.3
  168.0 0.0 copy-done
  168.0 2.7 %shard_map.114 = bf16[1024,512]{1,0:T(8,128)(2,1)} custom-call(bf16[128,8,512]{2,1,0:T(8,128)(2,1)S(1)} %all_to_all.21.recv_ref, f32[1024,512]{1,0:T(8,128)S(1)} %get-tuple-element.11.own_ref, bf16[1024,512]{1,0:T(8,128)(2,1)S(1)} %copy-done, f32[512,512]{1,0:T(8,128)S(1)} %get-tuple-element.12.self_ref), custom_call_target="tpu_custom_call" | custom-call | flops 1073741824 | bytes 6291456 | tf_op jit(solution)/shard_map/pallas_call | solution.py:196
  170.7 0.0 copy-start.5
  170.7 4.7 %all-to-all-start.2 = ((bf16[128,8,512]{2,1,0:T(8,128)(2,1)}), bf16[128,8,512]{2,1,0:T(8,128)(2,1)S(1)}, u32[]{:S(2)}, u32[]{:S(2)}) async-start(bf16[128,8,512]{2,1,0:T(8,128)(2,1)} %bitcast.1), calls=%async_computation.2 | async-start | bytes 2097152 | tf_op jit(solution)/shard_map/all_to_all | solution.py:272
  175.4 0.0 copy-done.5
  175.5 0.0 copy-start.1
  175.5 1.6 copy-done.1
  177.1 0.0 copy-start.2
  177.1 1.6 copy-done.2
  178.6 0.0 copy-start.4
  178.6 1.6 copy-done.4
  180.2 0.0 copy-start.6
  180.2 1.2 copy-done.6
  181.5 6.6 %shard_map.116 = f32[1024,512]{1,0:T(8,128)} custom-call(bf16[128,8,512]{2,1,0:T(8,128)(2,1)S(1)} %all_to_all.21.recv_ref, f32[1024,512]{1,0:T(8,128)S(1)} %copy-done.4, f32[1024,512]{1,0:T(8,128)S(1)} %copy-done.1, f32[1024,512]{1,0:T(8,128)S(1)} %copy-done.2, f32[512,512]{1,0:T(8,128)S(1)} %copy-done.5, f32[512,512]{1,0:T(8,128)S(1)} %copy-done.6), custom_call_target="tpu_custom_call" | custom-call | flops 3221225472 | bytes 10485760 | tf_op jit(solution)/shard_map/pallas_call | solution.py:242
  188.1 6.6 %all-to-all-done.2.shares_ref = bf16[128,8,512]{2,1,0:T(8,128)(2,1)S(1)} async-done(((bf16[128,8,512]{2,1,0:T(8,128)(2,1)}), bf16[128,8,512]{2,1,0:T(8,128)(2,1)S(1)}, u32[]{:S(2)}, u32[]{:S(2)}) %all-to-all-start.2) | async-done | bytes 1048608 | tf_op jit(solution)/shard_map/all_to_all | solution.py:272
  194.7 0.2 shard_map.115
  194.9 23.6 %all_to_all.22 = bf16[128,8,512]{2,1,0:T(8,128)(2,1)S(1)} all-to-all(bf16[128,8,512]{2,1,0:T(8,128)(2,1)S(1)} %shard_map.115), channel_id=1, replica_groups=mesh['nodes'=128] {'nodes'}, dimensions={0} | all-to-all | bytes 2097152 | tf_op jit(solution)/shard_map/all_to_all | solution.py:275
  218.5 1.6 multiply_bitcast_fusion
Async XLA Ops:
  16.5 151.5 %copy-start.3 = (f32[1024,512]{1,0:T(8,128)}, f32[1024,512]{1,0:T(8,128)S(1)}, u32[]{:S(2)}) copy-start(f32[1024,512]{1,0:T(8,128)S(1)} %get-tuple-element.11.own_ref) | copy-start | bytes 6291460
  142.2 25.8 %copy-start = (bf16[1024,512]{1,0:T(8,128)(2,1)S(1)}, bf16[1024,512]{1,0:T(8,128)(2,1)}, u32[]{:S(2)}) copy-start(bf16[1024,512]{1,0:T(8,128)(2,1)} %feat_ref.3) | copy-start | bytes 3145732
  170.7 4.7 %copy-start.5 = (f32[512,512]{1,0:T(8,128)S(1)}, f32[512,512]{1,0:T(8,128)}, u32[]{:S(2)}) copy-start(f32[512,512]{1,0:T(8,128)} %self_ref.1) | copy-start | bytes 3145732
  170.7 24.0 %all-to-all-start.2 = ((bf16[128,8,512]{2,1,0:T(8,128)(2,1)}), bf16[128,8,512]{2,1,0:T(8,128)(2,1)S(1)}, u32[]{:S(2)}, u32[]{:S(2)}) async-start(bf16[128,8,512]{2,1,0:T(8,128)(2,1)} %bitcast.1), calls=%async_computation.2 | async-start | bytes 2097152 | tf_op jit(solution)/shard_map/all_to_all | solution.py:272
  175.5 1.6 copy-start.1
  177.1 1.6 copy-start.2
  178.6 1.6 copy-start.4
  180.2 1.2 copy-start.6
